TPU v7x, 512 devices: a whole 4x4x16 slice. The times are simulated.
512 devices in a mesh: tok: 32 (over y, z_hi, x), tp: 16 (over z_lo, core).
Axes of the slice: x: 4, y: 4, z: 16 (z_hi: 2, z_lo: 8; z = z_hi * 8 + z_lo), core: 2. Of those that a mesh axis runs over, the one named last changes fastest.
Arguments:
- keys: bfloat16 [4, 1024, 8192], P(None, 'tok', 'tp'), may hold values from -6 to 6
- values: bfloat16 [4, 1024, 3072], P(None, 'tok', 'tp'), may hold values from -6 to 6
- cotangent: bfloat16 [4, 1024, 3072], P(None, 'tok'), may hold values from -0.09375 to 0.09375
- init_weight: bfloat16 [8192, 3072], P('tp'), may hold values from -0.0625 to 0.0625
Outputs:
- layer_out: bfloat16 [4, 1024, 3072], P(None, 'tok', 'tp')
- grad_init: bfloat16 [8192, 3072], P('tp', 'tok')
All inputs are finite; a program needn't handle non-finite values.
Results may differ from a plain program's by a relative error of at most 0.02.
Values may be sent and summed in bfloat16 or wider, within the bound.
A program may use at most 64 MiB of HBM per device.

v0:
```python
import math

import jax
import jax.numpy as jnp
from jax import lax
from jax.sharding import PartitionSpec as P

MOMENTUM = 0.9


def momentum_sum(count):
    return (1.0 - MOMENTUM**count) / (1.0 - MOMENTUM)


def weighted(block_scores, factors):
    table = jnp.asarray(factors, jnp.float32)[None, :, None]
    mb_rows = block_scores.shape[0]
    return (block_scores * table).astype(jnp.bfloat16).reshape(mb_rows, -1)


def per_device(keys, values, cotangent, init_weight):
    step_count, mb_rows, hidden_part = keys.shape
    model_width = init_weight.shape[1]
    tok_count = lax.axis_size("tok")
    tp_count = lax.axis_size("tp")
    batch_size = mb_rows * tok_count
    col_width = model_width // tp_count
    hidden = hidden_part * tp_count
    inner_rate = 0.5 * batch_size / (math.sqrt(hidden) + math.sqrt(batch_size)) ** 2
    step_scale = inner_rate / batch_size
    col_start = lax.axis_index("tp") * col_width
    gathered = lax.all_gather(keys, "tok", axis=1, tiled=True)
    score_table = lax.psum(
        jnp.einsum("tmf,sbf->tmsb", keys, gathered, preferred_element_type=jnp.float32), "tp"
    )
    key_rows = keys.reshape(step_count * mb_rows, hidden_part)
    partial_sum = jnp.dot(key_rows, init_weight, preferred_element_type=jnp.float32)
    projected_full = lax.psum(partial_sum, "tp")
    projected = lax.dynamic_slice_in_dim(projected_full, col_start, col_width, 1).reshape(
        step_count, mb_rows, col_width
    )
    residuals = []
    outputs = []
    for t in range(step_count):
        row_scores = score_table[t, :, : t + 1]
        residual = projected[t] - values[t].astype(jnp.float32)
        if t > 0:
            fwd_weights = weighted(
                row_scores[:, :t], [step_scale * momentum_sum(t - s) for s in range(t)]
            )
            earlier = jnp.concatenate(residuals, axis=0)
            residual = residual - jnp.dot(fwd_weights, earlier, preferred_element_type=jnp.float32)
        residual = residual.astype(jnp.bfloat16)
        residuals.append(lax.all_gather(residual, "tok", axis=0, tiled=True))
        out_weights = weighted(
            row_scores, [step_scale * momentum_sum(t + 1 - s) for s in range(t + 1)]
        )
        mixing = jnp.dot(
            out_weights, jnp.concatenate(residuals, axis=0), preferred_element_type=jnp.float32
        )
        outputs.append((projected[t] - mixing).astype(jnp.bfloat16))
    cotangent_part = lax.dynamic_slice_in_dim(cotangent, col_start, col_width, 2)
    cotangent_all = lax.all_gather(cotangent_part, "tok", axis=1, tiled=True)
    adjoint_all = [None] * step_count
    adjoint_local = [None] * step_count
    for s in reversed(range(step_count)):
        col_scores = score_table[s, :, s:]
        later_count = step_count - s
        out_weights = weighted(
            col_scores, [step_scale * momentum_sum(t + 1 - s) for t in range(s, step_count)]
        )
        accumulated = jnp.dot(
            out_weights,
            cotangent_all[s:].reshape(later_count * batch_size, col_width),
            preferred_element_type=jnp.float32,
        )
        if s + 1 < step_count:
            fwd_weights = weighted(
                col_scores[:, 1:],
                [step_scale * momentum_sum(t - s) for t in range(s + 1, step_count)],
            )
            later = jnp.concatenate(adjoint_all[s + 1 :], axis=0)
            accumulated = accumulated + jnp.dot(
                fwd_weights, later, preferred_element_type=jnp.float32
            )
        adjoint = (-accumulated).astype(jnp.bfloat16)
        adjoint_local[s] = adjoint
        if s > 0:
            adjoint_all[s] = lax.all_gather(adjoint, "tok", axis=0, tiled=True)
    adjoint_full = lax.all_gather(jnp.stack(adjoint_local), "tp", axis=2, tiled=True)
    adjoint_sum = adjoint_full.astype(jnp.float32) + cotangent.astype(jnp.float32)
    partial_grad = lax.dot_general(
        key_rows.astype(jnp.float32),
        adjoint_sum.reshape(step_count * mb_rows, model_width),
        (((0,), (0,)), ((), ())),
        precision=lax.Precision.HIGHEST,
        preferred_element_type=jnp.float32,
    )
    grad_sum = lax.psum_scatter(
        partial_grad.astype(jnp.bfloat16), "tok", scatter_dimension=1, tiled=True
    )
    return (jnp.stack(outputs), grad_sum)


def solution(mesh):
    return jax.shard_map(
        per_device,
        mesh=mesh,
        in_specs=(P(None, "tok", "tp"), P(None, "tok", "tp"), P(None, "tok", None), P("tp", None)),
        out_specs=(P(None, "tok", "tp"), P("tp", "tok")),
        check_vma=False,
    )
```

profile of v0, /device:TPU:2, one launch (start us, length us, event | category | flops | bytes accessed | tf_op | source)
XLA Modules:
  0.0 1684.7 jit_solution(12963843057370209042)
XLA Ops:
  9.1 2.7 fusion.105
  11.8 177.1 %all-gather.3.cloned.1.call-done = bf16[4,1024,512]{2,1,0:T(8,128)(2,1)} async-done(((bf16[4,32,512]{2,1,0:T(8,128)(2,1)}), bf16[4,1024,512]{2,1,0:T(8,128)(2,1)}) %all-gather.3.cloned.1.call-update) | async-done | bytes 4194320 | tf_op jit(solution)/shard_map/all_gather | solution.py:32
  188.9 5.0 fusion
  194.0 1.6 constant_dynamic-slice_fusion
  195.7 203.4 %all-reduce.3.cloned.1.call-done = (f32[4,32,4,1024]{3,1,2,0:T(8,128)}, f32[128,3072]{1,0:T(8,128)}) async-done(((f32[4,32,4,1024]{3,1,2,0:T(8,128)}, f32[128,3072]{1,0:T(8,128)}), (f32[4,32,4,1024]{3,1,2,0:T(8,128)}, f32[128,3072]{1,0:T(8,128)})) %all-reduce.3.cloned.1.call-update) | async-done | bytes 3670032 | tf_op jit(solution)/shard_map/psum | solution.py:33
  399.0 2.1 slice_bitcast_fusion.4
  401.1 2.1 slice_bitcast_fusion.3
  403.2 1.3 slice_bitcast_fusion.2
  404.6 130.2 %all-gather.5.cloned.1.call-done = bf16[4,1024,192]{2,1,0:T(8,128)(2,1)} async-done(((bf16[4,32,192]{2,1,0:T(8,128)(2,1)}), bf16[4,1024,192]{2,1,0:T(8,128)(2,1)}) %all-gather.5.cloned.1.call-update) | async-done | bytes 1572880 | tf_op jit(solution)/shard_map/all_gather | solution.py:63
  534.7 1.4 fusion.51
  536.2 149.7 %all_gather.36 = bf16[1024,192]{1,0:T(8,128)(2,1)S(1)} all-gather(bf16[32,192]{1,0:T(8,128)(2,1)S(1)} %fusion.51), channel_id=1, replica_groups=mesh['tok'=32,'tp'=16] {'tok'}, dimensions={0}, use_global_device_ids=true | all-gather | bytes 405504 | tf_op jit(solution)/shard_map/all_gather | solution.py:89
  687.0 1.8 fusion.44
  688.8 148.9 %all_gather.37 = bf16[1024,192]{1,0:T(8,128)(2,1)S(1)} all-gather(bf16[32,192]{1,0:T(8,128)(2,1)S(1)} %fusion.44), channel_id=1, replica_groups=mesh['tok'=32,'tp'=16] {'tok'}, dimensions={0}, use_global_device_ids=true | all-gather | bytes 405504 | tf_op jit(solution)/shard_map/all_gather | solution.py:89
  839.4 1.4 fusion.28
  841.1 150.0 %all_gather.38 = bf16[1024,192]{1,0:T(8,128)(2,1)S(1)} all-gather(bf16[32,192]{1,0:T(8,128)(2,1)S(1)} %fusion.45), channel_id=1, replica_groups=mesh['tok'=32,'tp'=16] {'tok'}, dimensions={0}, use_global_device_ids=true | all-gather | bytes 405504 | tf_op jit(solution)/shard_map/all_gather | solution.py:89
  991.1 1.5 convolution_bitcast_fusion.1
  993.6 1.7 copy.94
  995.3 48.4 %all_gather.39 = bf16[4,32,3072]{1,0,2:T(4,128)(2,1)} all-gather(bf16[4,32,192]{1,0,2:T(4,128)(2,1)} %copy.94), channel_id=1, replica_groups=mesh['tok'=32,'tp'=16] {'tp'}, dimensions={2}, use_global_device_ids=true | all-gather | bytes 835584 | tf_op jit(solution)/shard_map/all_gather | solution.py:90
  1043.7 5.0 copy.95
  1048.6 5.7 fusion.2
  1062.3 150.7 %all_gather.31 = bf16[1024,192]{1,0:T(8,128)(2,1)S(1)} all-gather(bf16[32,192]{1,0:T(8,128)(2,1)S(1)} %fusion.97), channel_id=1, replica_groups=mesh['tok'=32,'tp'=16] {'tok'}, dimensions={0}, use_global_device_ids=true | all-gather | bytes 405504 | tf_op jit(solution)/shard_map/all_gather | solution.py:54
  1214.1 150.6 %all_gather.32 = bf16[1024,192]{1,0:T(8,128)(2,1)S(1)} all-gather(bf16[32,192]{1,0:T(8,128)(2,1)S(1)} %fusion.50), channel_id=1, replica_groups=mesh['tok'=32,'tp'=16] {'tok'}, dimensions={0}, use_global_device_ids=true | all-gather | bytes 405504 | tf_op jit(solution)/shard_map/all_gather | solution.py:54
  1366.0 157.7 %all_gather.33 = bf16[1024,192]{1,0:T(8,128)(2,1)S(1)} all-gather(bf16[32,192]{1,0:T(8,128)(2,1)S(1)} %fusion.41), channel_id=1, replica_groups=mesh['tok'=32,'tp'=16] {'tok'}, dimensions={0}, use_global_device_ids=true | all-gather | bytes 405504 | tf_op jit(solution)/shard_map/all_gather | solution.py:54
  1527.1 148.0 %all_gather.34 = bf16[1024,192]{1,0:T(8,128)(2,1)S(1)} all-gather(bf16[32,192]{1,0:T(8,128)(2,1)S(1)} %fusion.43), channel_id=1, replica_groups=mesh['tok'=32,'tp'=16] {'tok'}, dimensions={0}, use_global_device_ids=true | all-gather | bytes 405504 | tf_op jit(solution)/shard_map/all_gather | solution.py:54
  (83 shorter events, 22.7 us)
Async XLA Ops:
  7.2 1.9 copy-start
  7.2 181.7 %all-gather.3.cloned.1.call-start = ((), (), s32[]{:S(2)}) async-start(), calls=%async_computation.1 | async-start | bytes 4325376 | tf_op jit(solution)/shard_map/all_gather | solution.py:32
  7.9 391.1 %all-reduce.3.cloned.1.call-start = ((), (), s32[]{:S(2)}) async-start(), calls=%async_computation.4 | async-start | bytes 7340032 | tf_op jit(solution)/shard_map/psum | solution.py:33
  9.1 179.8 %copy-start.9 = (bf16[4,32,512]{2,1,0:T(8,128)(2,1)S(1)}, bf16[4,32,512]{2,1,0:T(8,128)(2,1)}, u32[]{:S(2)}) copy-start(bf16[4,32,512]{2,1,0:T(8,128)(2,1)} %param.18) | copy-start | bytes 393220
  193.9 340.8 %all-gather.5.cloned.1.call-start = ((), (), s32[]{:S(2)}) async-start(), calls=%async_computation.2 | async-start | bytes 2162688 | tf_op jit(solution)/shard_map/all_gather | solution.py:63
  195.6 1482.6 %reduce-scatter.2.cloned.1.call-start = ((), (), s32[]{:S(2)}) async-start(), calls=%async_computation.3 | async-start | bytes 3244032 | tf_op jit(solution)/shard_map/reduce_scatter | solution.py:99
  399.0 4.2 copy-start.2
  403.2 283.8 %copy-start.14 = (f32[2]{0:T(128)S(1)}, f32[2]{0:T(128)}, u32[]{:S(2)}) copy-start(f32[2]{0:T(128)} %constant.28.clone) | copy-start | bytes 28
  404.6 433.2 %copy-start.17 = (f32[2]{0:T(128)S(1)}, f32[2]{0:T(128)}, u32[]{:S(2)}) copy-start(f32[2]{0:T(128)} %constant.25.clone) | copy-start | bytes 28
  534.7 303.0 %copy-start.6 = (f32[32,3,1024]{2,0,1:T(8,128)S(1)}, f32[32,3,1024]{2,0,1:T(8,128)}, u32[]{:S(2)}) copy-start(f32[32,3,1024]{2,0,1:T(8,128)} %get-tuple-element.11) | copy-start | bytes 1179652
  534.7 303.0 %copy-start.7 = (f32[32,3,1024]{2,0,1:T(8,128)S(1)}, f32[32,3,1024]{2,0,1:T(8,128)}, u32[]{:S(2)}) copy-start(f32[32,3,1024]{2,0,1:T(8,128)} %get-tuple-element.12) | copy-start | bytes 1179652
  536.1 302.4 %copy-start.4 = (f32[32,4,1024]{2,0,1:T(8,128)S(1)}, f32[32,4,1024]{2,0,1:T(8,128)}, u32[]{:S(2)}) copy-start(f32[32,4,1024]{2,0,1:T(8,128)} %get-tuple-element.8) | copy-start | bytes 1572868
  536.1 302.4 %copy-start.5 = (f32[32,4,1024]{2,0,1:T(8,128)S(1)}, f32[32,4,1024]{2,0,1:T(8,128)}, u32[]{:S(2)}) copy-start(f32[32,4,1024]{2,0,1:T(8,128)} %get-tuple-element.9) | copy-start | bytes 1572868
  536.1 302.4 %copy-start.15 = (f32[3]{0:T(128)S(1)}, f32[3]{0:T(128)}, u32[]{:S(2)}) copy-start(f32[3]{0:T(128)} %constant.29.clone) | copy-start | bytes 40
  536.2 302.4 %copy-start.16 = (f32[3]{0:T(128)S(1)}, f32[3]{0:T(128)}, u32[]{:S(2)}) copy-start(f32[3]{0:T(128)} %constant.26.clone) | copy-start | bytes 40
  687.0 152.4 %copy-start.1 = (bf16[4,1024,192]{2,1,0:T(8,128)(2,1)S(1)}, bf16[4,1024,192]{2,1,0:T(8,128)(2,1)}, u32[]{:S(2)}) copy-start(bf16[4,1024,192]{2,1,0:T(8,128)(2,1)} %all-gather.5.cloned.1.call-done) | copy-start | bytes 4718596
  839.4 151.7 %copy-start.18 = (f32[4]{0:T(128)S(1)}, f32[4]{0:T(128)}, u32[]{:S(2)}) copy-start(f32[4]{0:T(128)} %constant.30.clone) | copy-start | bytes 52
  1054.3 0.7 copy-start.19
  1057.0 3.7 copy-start.3
  1059.3 2.2 copy-start.10
  1060.8 152.4 %copy-start.8 = (f32[32,2,1024]{2,0,1:T(8,128)S(1)}, f32[32,2,1024]{2,0,1:T(8,128)}, u32[]{:S(2)}) copy-start(f32[32,2,1024]{2,0,1:T(8,128)} %get-tuple-element.15) | copy-start | bytes 786436
  1364.8 160.0 %copy-start.12 = (f32[1,8,2,128]{3,1,2,0:T(8,128)S(1)}, f32[1,8,2,128]{3,1,2,0:T(8,128)}, u32[]{:S(2)}) copy-start(f32[1,8,2,128]{3,1,2,0:T(8,128)} %copy.112) | copy-start | bytes 24580
  1523.7 151.4 %copy-start.11 = (f32[3072]{0:T(1024)S(1)}, f32[3072]{0:T(1024)}, u32[]{:S(2)}) copy-start(f32[3072]{0:T(1024)} %mul.158) | copy-start | bytes 36868
  1525.9 150.3 %copy-start.13 = (f32[1,8,4,128]{3,1,2,0:T(8,128)S(1)}, f32[1,8,4,128]{3,1,2,0:T(8,128)}, u32[]{:S(2)}) copy-start(f32[1,8,4,128]{3,1,2,0:T(8,128)} %copy.111) | copy-start | bytes 49156
Sparse Core Ops, SparseCore 0:
  12.3 176.5 all-gather.2
  194.0 204.9 all-reduce.2
  403.9 130.7 all-gather.4
  1054.4 317.8 reduce-scatter.1
where the time goes:
time: 1690 us; the launch traced here: 1680 us
  blocking collectives  1100 us (65%)
  waiting for transfers between devices  511 us (30%)
  matrix products  29 us (2%)
  local copies, waits for them, and re-layouts  22.2 us (1%)
    all_gather x4, blocking collectives, per_device(): residuals.append(lax.all_gather(residual, 'tok', axis=0, tiled=True))  607 us
    all_gather x3, blocking collectives, per_device(): adjoint_all[s] = lax.all_gather(adjoint, 'tok', axis=0, tiled=True)  449 us
    psum x1, waiting for transfers between devices, per_device(): lax.psum(jnp.einsum('tmf,sbf->tmsb', keys, gathered, preferred_element_ty...  203 us
    all_gather x1, waiting for transfers between devices, per_device(): gathered = lax.all_gather(keys, 'tok', axis=1, tiled=True)  177 us
    all_gather x1, waiting for transfers between devices, per_device(): cotangent_all = lax.all_gather(cotangent_part, 'tok', axis=1, tiled=True)  130 us
    all_gather x1, blocking collectives, per_device(): lax.all_gather(jnp.stack(adjoint_local), 'tp', axis=2, tiled=True)  48.4 us
  transfers between devices with their start and end apart: 4, of which 3 were waited for; matrix products, arithmetic and copies ran while one was open for 2% of the time, Pallas kernels for 0%

commit v1 on v0

v1 whole, which is shorter than its diff:
```python
import functools
import math

import jax
import jax.numpy as jnp
from jax import lax
from jax.experimental import pallas as pl
from jax.experimental.pallas import tpu as pltpu
from jax.sharding import PartitionSpec as P

MOMENTUM = 0.9
LANES = 128
F32 = jnp.float32
BF16 = jnp.bfloat16
VMEM_LIMIT = 48 * 1024 * 1024


def momentum_sum(count):
    return (1.0 - MOMENTUM**count) / (1.0 - MOMENTUM)


class Grid:
    def __init__(self, side, depth):
        self.side, self.depth, self.area = side, depth, side * side
        tok, tp = lax.axis_index("tok"), lax.axis_index("tp")
        self.tok, self.tp = tok, tp
        self.y = lax.div(tok, 2 * side)
        self.zhi = lax.rem(lax.div(tok, side), 2)
        self.x = lax.rem(tok, side)
        self.zlo = lax.div(tp, 2)
        self.core = lax.rem(tp, 2)
        self.a = self.y * side + self.x
        self.z = self.zhi * depth + self.zlo

    def tok_of(self, y, zhi, x):
        return y * (2 * self.side) + zhi * self.side + x

    def at_xy(self, dy, dx):
        y = lax.rem(self.y + dy + self.side, self.side)
        x = lax.rem(self.x + dx + self.side, self.side)
        return (self.tok_of(y, self.zhi, x), self.tp)

    def a_at(self, dy, dx):
        y = lax.rem(self.y + dy + self.side, self.side)
        x = lax.rem(self.x + dx + self.side, self.side)
        return y * self.side + x

    def partner(self):
        return (self.tok_of(self.y, 1 - self.zhi, self.x), self.tp)

    def sibling(self):
        return (self.tok, self.zlo * 2 + 1 - self.core)

    def zlo_at(self, d):
        return lax.rem(self.zlo + d + self.depth, self.depth)

    def on_line(self, d):
        return (self.tok, self.zlo_at(d) * 2 + self.core)

    def z_at(self, d):
        return lax.rem(self.z + d + 2 * self.depth, 2 * self.depth)

    def on_ring(self, d):
        z = self.z_at(d)
        zhi, zlo = lax.div(z, self.depth), lax.rem(z, self.depth)
        return (self.tok_of(self.y, zhi, self.x), zlo * 2 + self.core)

    def xy_offsets(self):
        return [(dy, dx) for dy in range(self.side) for dx in range(self.side) if (dy, dx) != (0, 0)]

    def line_order(self):
        half = self.depth // 2
        return sorted(range(1, self.depth), key=lambda d: abs(d - half)) + [0]


def remote(src, dst, send, recv, device):
    return pltpu.make_async_remote_copy(
        src_ref=src, dst_ref=dst, send_sem=send, recv_sem=recv, device_id=device, device_id_type=pl.DeviceIdType.MESH
    )


def greet(targets, count):
    barrier = pltpu.get_barrier_semaphore()
    for device in targets:
        pl.semaphore_signal(barrier, inc=1, device_id=device, device_id_type=pl.DeviceIdType.MESH)
    pl.semaphore_wait(barrier, count)


class Wave:
    def __init__(self, grid, blocks, sems):
        side, steps = grid.side, blocks.shape[0]
        half = steps // 2
        self.first, self.second = {}, {}
        send1, recv1, send2, recv2 = sems
        for h in range(2):
            part = pl.ds(h * half, half)
            for d in range(1, side):
                mine = blocks.at[part, grid.a]
                peer = grid.at_xy(d, 0) if h == 0 else grid.at_xy(0, d)
                self.first[h, d] = remote(mine, mine, send1.at[h, d], recv1.at[h, d], peer)
            for d in range(side):
                held = blocks.at[part, grid.a_at(-d, 0) if h == 0 else grid.a_at(0, -d)]
                for e in range(1, side):
                    peer = grid.at_xy(0, e) if h == 0 else grid.at_xy(e, 0)
                    self.second[h, d, e] = remote(held, held, send2.at[h, d, e], recv2.at[h, d, e], peer)
        self.side = side

    def start(self):
        for d in range(1, self.side):
            for h in range(2):
                self.first[h, d].start()
        for e in range(1, self.side):
            for h in range(2):
                self.second[h, 0, e].start()

    def forward(self):
        for d in range(1, self.side):
            for h in range(2):
                self.first[h, d].wait_recv()
                for e in range(1, self.side):
                    self.second[h, d, e].start()

    def finish(self):
        for copy in self.second.values():
            copy.wait_recv()
        for copy in list(self.first.values()) + list(self.second.values()):
            copy.wait_send()


def wave_scratch(side):
    return [pltpu.SemaphoreType.DMA((2, side))] * 2 + [pltpu.SemaphoreType.DMA((2, side, side))] * 2


class LineSum:
    def __init__(self, grid, part, sib_in, stage, recv, sems):
        self.grid, self.part, self.sib_in, self.stage, self.recv = grid, part, sib_in, stage, recv
        sib_send, sib_recv, send, rsem = sems
        self.order = grid.line_order()
        self.sib, self.line = {}, {}
        for d in self.order:
            theirs = part.at[grid.zlo_at(d) * 2 + 1 - grid.core]
            self.sib[d] = remote(theirs, sib_in.at[d], sib_send.at[d], sib_recv.at[d], grid.sibling())
            if d:
                self.line[d] = remote(stage.at[d], recv.at[d], send.at[d], rsem.at[d], grid.on_line(d))

    def pair(self, d):
        own = self.part[self.grid.zlo_at(d) * 2 + self.grid.core]
        return own.astype(F32) + self.sib_in[d].astype(F32)

    def send(self):
        for d in self.order:
            self.sib[d].wait_recv()
            if d:
                self.stage[d] = self.pair(d).astype(BF16)
                self.line[d].start()

    def total(self):
        total = self.pair(0)
        for d in self.order[:-1]:
            self.line[d].wait_recv()
            total = total + self.recv[d].astype(F32)
        return total

    def finish(self):
        for copy in list(self.sib.values()) + list(self.line.values()):
            copy.wait_send()


def line_scratch(depth, rows):
    return [
        pltpu.VMEM((depth, rows, LANES), BF16),
        pltpu.VMEM((depth, rows, LANES), BF16),
        pltpu.VMEM((depth, rows, LANES), BF16),
    ] + [pltpu.SemaphoreType.DMA((depth,))] * 4


def line_devices(grid):
    return [grid.sibling()] + [grid.on_line(d) for d in range(1, grid.depth)]


def gather_kernel(
    side, depth, key_ref, part_ref, vc_ref, kmine, kpair, call, pm, vm,
    total_ref, vc_in, sib_in, stage, recv, ls0, ls1, ls2, ls3, w0, w1, w2, w3, swap_sem, c_send, c_recv,
):
    grid = Grid(side, depth)
    zhi = grid.zhi
    xy = grid.xy_offsets()
    targets = [grid.partner()] + [grid.at_xy(*d) for d in xy] + line_devices(grid)
    greet(targets, len(targets))

    lines = LineSum(grid, part_ref, sib_in, stage, recv, (ls0, ls1, ls2, ls3))
    for d in lines.order:
        lines.sib[d].start()
    vc_swap = remote(vc_ref.at[1 - zhi], vc_in, swap_sem.at[0, 0], swap_sem.at[1, 0], grid.partner())
    vc_swap.start()
    key_swap = remote(key_ref, kpair, swap_sem.at[0, 1], swap_sem.at[1, 1], grid.partner())
    key_swap.start()
    kmine[:, grid.a] = key_ref[...]
    wave = Wave(grid, kmine, (w0, w1, w2, w3))
    wave.start()
    lines.send()
    wave.forward()

    vc_swap.wait()
    vm[zhi] = vc_ref[zhi, 0]
    vm[1 - zhi] = vc_in[0]
    call[:, zhi, grid.a] = vc_ref[zhi, 1]
    call[:, 1 - zhi, grid.a] = vc_in[1]
    mine = call.at[:, :, grid.a]
    spread = [remote(mine, mine, c_send.at[dy, dx], c_recv.at[dy, dx], grid.at_xy(dy, dx)) for dy, dx in xy]
    for copy in spread:
        copy.start()

    total_ref[...] = lines.total().reshape(total_ref.shape)
    pm[zhi] = total_ref[zhi]
    p_swap = remote(total_ref.at[1 - zhi], pm.at[zhi], swap_sem.at[0, 2], swap_sem.at[1, 2], grid.partner())
    p_swap.start()

    for copy in spread:
        copy.wait()
    wave.finish()
    lines.finish()
    key_swap.wait()
    p_swap.wait()


def scores_kernel(
    side, depth, kmine, kpair, kother, sall,
    lhs, part, sib_in, stage, recv, ls0, ls1, ls2, ls3, w0, w1, w2, w3, ring_send, ring_recv, sib_send, sib_recv,
):
    grid = Grid(side, depth)
    zhi = grid.zhi
    targets = [grid.at_xy(d, 0) for d in range(1, side)] + [grid.at_xy(0, d) for d in range(1, side)]
    targets += line_devices(grid) + [grid.on_ring(1), grid.on_ring(-1)]
    greet(targets, len(targets))

    kother[:, grid.a] = kpair[...]
    wave = Wave(grid, kother, (w0, w1, w2, w3))
    wave.start()

    quarters = kmine.shape[1] * kmine.shape[2] // LANES
    width = kmine.shape[3]
    lhs[zhi] = kmine[:, grid.a]
    lhs[1 - zhi] = kpair[...]
    rows = lhs[...].reshape(-1, width)
    lines = LineSum(grid, part, sib_in, stage, recv, (ls0, ls1, ls2, ls3))

    def piece(j):
        s, q = lax.div(j, quarters), lax.rem(j, quarters)
        block = kmine[s, pl.ds(q * 4, 4)].reshape(LANES, width)
        part[j] = lax.dot_general(
            rows, block, (((1,), (1,)), ((), ())), preferred_element_type=F32
        ).astype(BF16)

    for d in lines.order:
        piece(grid.zlo_at(d) * 2 + 1 - grid.core)
        lines.sib[d].start()
    for d in lines.order:
        piece(grid.zlo_at(d) * 2 + grid.core)
    lines.send()
    wave.forward()

    def columns(z):
        half, j = lax.div(z, depth), lax.rem(z, depth) * 2 + grid.core
        s, q = lax.div(j, quarters), lax.rem(j, quarters)
        return sall.at[:, pl.ds(pl.multiple_of((s * 2 + half) * quarters * LANES + q * LANES, LANES), LANES)]

    total = lines.total()
    mine = columns(grid.z)
    mine[...] = total.astype(BF16)

    def hop(step, way):
        held = columns(grid.z_at(-way * step))
        slot = 0 if way > 0 else 1
        return remote(held, held, ring_send.at[slot, step], ring_recv.at[slot, step], grid.on_ring(way))

    def share(z, slot):
        held = columns(z)
        return remote(held, held, sib_send.at[slot], sib_recv.at[slot], grid.sibling())

    copies, shared = [], []

    def go(copy, to):
        copy.start()
        to.append(copy)

    up, down = hop(0, 1), hop(0, -1)
    go(up, copies)
    go(down, copies)
    go(share(grid.z, 0), shared)
    for step in range(depth):
        up.wait_recv()
        if step + 1 < depth:
            up = hop(step + 1, 1)
            go(up, copies)
            down.wait_recv()
            if step + 2 < depth:
                down = hop(step + 1, -1)
                go(down, copies)
        go(share(grid.z_at(-step - 1), 1 + step), shared)
        if step + 1 < depth:
            go(share(grid.z_at(step + 1), 1 + depth + step), shared)
    for copy in shared:
        copy.wait()
    for copy in copies:
        copy.wait_send()
    wave.finish()
    lines.finish()


def rounds_kernel(
    side, depth, scale, sall, pm, vm, call, out, comb,
    msg, xg, acc_f, acc_o, acc_b, tsend, osend,
    x_send, x_recv, t_send, t_recv, l_send, l_recv, s_send, s_recv, o_send, o_recv,
):
    grid = Grid(side, depth)
    zhi, area = grid.zhi, grid.area
    steps = pm.shape[1]
    mb = pm.shape[2]
    xy = grid.xy_offsets()
    holder = (2 * grid.tp + zhi, lax.rem(grid.a + area // 2, area))
    source_tp = lax.div(grid.tok, 2)
    source_a = lax.rem(grid.tp + area // 2, area)
    source = (grid.tok_of(lax.div(source_a, side), lax.rem(grid.tok, 2), lax.rem(source_a, side)), source_tp)
    near = [grid.at_xy(*d) for d in xy] + line_devices(grid) + [grid.partner()]
    greet(near + [source], len(near) + 1)

    scores = sall[...]
    batch = 2 * area * mb

    def product(column, right):
        return jnp.dot(
            scores[:, column * batch:(column + 1) * batch], right.reshape(batch, LANES), preferred_element_type=F32
        ).reshape(2, steps, mb, LANES)

    acc_f[...] = jnp.zeros_like(acc_f)
    acc_o[...] = jnp.zeros_like(acc_o)
    acc_b[...] = jnp.zeros_like(acc_b)

    def from_cotangent(t):
        term = product(t, call[t])
        for s in range(t + 1):
            acc_b[:, s] += (scale * momentum_sum(t + 1 - s)) * term[:, s]

    def line_copies(u):
        slot = comb.at[u, :, source_a]
        out_copies = [
            remote(slot, slot, l_send.at[u, d], l_recv.at[u, d], grid.on_line(d)) for d in range(1, depth)
        ]
        shares = []
        for d in range(depth):
            a = lax.rem(grid.zlo_at(-d) * 2 + grid.core + area // 2, area)
            held = comb.at[u, :, a]
            shares.append(remote(held, held, s_send.at[u, d], s_recv.at[u, d], grid.sibling()))
        return out_copies, shares

    to_holder, lines, shares, spread, given = {}, {}, {}, {}, {}
    from_cotangent(steps - 1)
    for r in range(steps):
        t, u = r, steps - 1 - r
        msg[r, 0] = (pm[:, t] - acc_f[:, t] - vm[:, t].astype(F32)).astype(BF16)
        adjoint = (-acc_b[:, u]).astype(BF16)
        msg[r, 1] = adjoint
        spread[r] = [
            remote(msg.at[r], xg.at[r, :, :, grid.a], x_send.at[r, dy, dx], x_recv.at[r, dy, dx], grid.at_xy(dy, dx))
            for dy, dx in xy
        ]
        for copy in spread[r]:
            copy.start()
        tsend[u] = (adjoint.astype(F32) + call[u, :, grid.a].astype(F32)).astype(BF16)
        to_holder[u] = remote(tsend.at[u], comb.at[u, :, grid.a], t_send.at[u], t_recv.at[u], holder)
        to_holder[u].start()
        xg[r, :, :, grid.a] = msg[r]
        if u > 0:
            from_cotangent(u - 1)
        if r > 0:
            to_holder[u + 1].wait_recv()
            lines[u + 1], shares[u + 1] = line_copies(u + 1)
            for copy in lines[u + 1]:
                copy.start()
            shares[u + 1][0].start()
        if r > 1:
            for d in range(1, depth):
                lines[u + 2][d - 1].wait_recv()
                shares[u + 2][d].start()
        for copy in spread[r]:
            copy.wait_recv()
        forward = product(t, xg[r, 0])
        for row in range(t, steps):
            if row > t:
                acc_f[:, row] += (scale * momentum_sum(row - t)) * forward[:, row]
            acc_o[:, row] += (scale * momentum_sum(row + 1 - t)) * forward[:, row]
        if u > 0:
            backward = product(u, xg[r, 1])
            for row in range(u):
                acc_b[:, row] += (scale * momentum_sum(u - row)) * backward[:, row]
        result = (pm[:, t] - acc_o[:, t]).astype(BF16)
        osend[:, t] = result
        out[zhi, t] = osend[zhi, t]
        given[t] = remote(osend.at[1 - zhi, t], out.at[zhi, t], o_send.at[t], o_recv.at[t], grid.partner())
        given[t].start()

    to_holder[0].wait_recv()
    lines[0], shares[0] = line_copies(0)
    for copy in lines[0]:
        copy.start()
    shares[0][0].start()
    for u in (1, 0):
        for d in range(1, depth):
            lines[u][d - 1].wait_recv()
            shares[u][d].start()
    for u in range(steps):
        for copy in shares[u]:
            copy.wait()
        for copy in lines[u] + spread[u]:
            copy.wait_send()
        to_holder[u].wait_send()
        given[u].wait()


def call_kernel(body, name, identity, outs, scratch, *args):
    vmem = pl.BlockSpec(memory_space=pltpu.VMEM)
    return pl.pallas_call(
        body,
        name=name,
        out_shape=[jax.ShapeDtypeStruct(shape, dtype) for shape, dtype in outs],
        in_specs=[vmem] * len(args),
        out_specs=[vmem] * len(outs),
        scratch_shapes=scratch,
        compiler_params=pltpu.CompilerParams(
            collective_id=identity, has_side_effects=True, vmem_limit_bytes=VMEM_LIMIT
        ),
    )(*args)


def per_device(keys, values, cotangent, init_weight):
    steps, mb, width = keys.shape
    model_width = init_weight.shape[1]
    tok_count, tp_count = lax.axis_size("tok"), lax.axis_size("tp")
    side, depth = math.isqrt(tok_count // 2), tp_count // 2
    area = side * side
    rows = steps * mb
    cols = model_width // (2 * tp_count)
    hidden, batch_size = width * tp_count, mb * tok_count
    inner_rate = 0.5 * batch_size / (math.sqrt(hidden) + math.sqrt(batch_size)) ** 2
    scale = inner_rate / batch_size
    tp = lax.axis_index("tp")
    zhi = lax.rem(lax.div(lax.axis_index("tok"), side), 2)
    dma = pltpu.SemaphoreType.DMA

    def pad(array):
        return jnp.pad(array, [(0, 0)] * (array.ndim - 1) + [(0, LANES - cols)])

    key_rows = keys.reshape(rows, width)
    projected = jnp.dot(key_rows, init_weight, preferred_element_type=F32).astype(BF16)
    projected = pad(projected.reshape(rows, tp_count, 2, cols).transpose(1, 2, 0, 3))
    projected = projected.reshape(tp_count, 2 * rows, LANES)
    cot = lax.dynamic_slice_in_dim(cotangent, tp * 2 * cols, 2 * cols, 2)
    vc = jnp.stack([values, cot]).reshape(2, steps, mb, 2, cols).transpose(3, 0, 1, 2, 4)
    vc = pad(vc)

    kmine, kpair, call, pm, vm = call_kernel(
        functools.partial(gather_kernel, side, depth), "gather", 0,
        [
            ((steps, area, mb, width), BF16), ((steps, mb, width), BF16), ((steps, 2, area, mb, LANES), BF16),
            ((2, steps, mb, LANES), F32), ((2, steps, mb, LANES), BF16),
        ],
        [pltpu.VMEM((2, steps, mb, LANES), F32), pltpu.VMEM((2, steps, mb, LANES), BF16)]
        + line_scratch(depth, 2 * rows) + wave_scratch(side) + [dma((2, 3)), dma((side, side)), dma((side, side))],
        keys, projected, vc,
    )
    kother, sall = call_kernel(
        functools.partial(scores_kernel, side, depth), "scores", 1,
        [((steps, area, mb, width), BF16), ((2 * rows, steps * batch_size), BF16)],
        [pltpu.VMEM((2, steps, mb, width), BF16), pltpu.VMEM((tp_count, 2 * rows, LANES), BF16)]
        + line_scratch(depth, 2 * rows) + wave_scratch(side)
        + [dma((2, depth)), dma((2, depth)), dma((2 * depth,)), dma((2 * depth,))],
        kmine, kpair,
    )
    half = (2, steps, mb, LANES)
    out, comb = call_kernel(
        functools.partial(rounds_kernel, side, depth, scale), "rounds", 2,
        [(half, BF16), ((steps, 2, area, mb, LANES), BF16)],
        [
            pltpu.VMEM((steps, 2, 2, mb, LANES), BF16), pltpu.VMEM((steps, 2, 2, area, mb, LANES), BF16),
            pltpu.VMEM(half, F32), pltpu.VMEM(half, F32), pltpu.VMEM(half, F32),
            pltpu.VMEM((steps, 2, mb, LANES), BF16), pltpu.VMEM(half, BF16),
            dma((steps, side, side)), dma((steps, side, side)), dma((steps,)), dma((steps,)),
            dma((steps, depth)), dma((steps, depth)), dma((steps, depth)), dma((steps, depth)),
            dma((steps,)), dma((steps,)),
        ],
        sall, pm, vm, call,
    )
    layer_out = out[..., :cols].transpose(1, 2, 0, 3).reshape(steps, mb, 2 * cols)

    def gradient(blocks, which):
        right = lax.dynamic_index_in_dim(comb, which, 1, keepdims=False).reshape(-1, LANES)[:, :cols]
        return lax.dot_general(
            blocks.reshape(-1, width), right, (((0,), (0,)), ((), ())), preferred_element_type=F32
        )

    grad = gradient(kmine, zhi) + gradient(kother, 1 - zhi)
    return (layer_out, grad.astype(BF16))


def solution(mesh):
    return jax.shard_map(
        per_device,
        mesh=mesh,
        in_specs=(P(None, "tok", "tp"), P(None, "tok", "tp"), P(None, "tok", None), P("tp", None)),
        out_specs=(P(None, "tok", "tp"), P("tp", "tok")),
        check_vma=False,
    )
```

time: 1690 us -> 213 us (0.13)
  the two profiles are of different devices: /device:TPU:2 before, /device:TPU:1 now
where the time goes in v1:
time: 213 us; the launch traced here: 211 us
  Pallas kernels  188 us (88%)
  local copies, waits for them, and re-layouts  17.9 us (8%)
  matrix products  3.94 us (2%)
    pallas_call x3, Pallas kernels, call_kernel(): pl.pallas_call(body, name=name, out_shape=[jax.ShapeDtypeStruct(shape, dt...  188 us
    unnamed x19, local copies, waits for them, and re-layouts  9.58 us

profile of v1, /device:TPU:1, one launch (start us, length us, event | category | flops | bytes accessed | tf_op | source)
XLA Modules:
  0.0 210.7 jit_solution(12182483308576043608)
XLA Ops:
  0.6 0.0 copy-start
  0.6 1.9 copy-done
  2.5 2.4 %convolution_convert_fusion = bf16[128,3072]{1,0:T(8,128)(2,1)} fusion(bf16[128,512]{1,0:T(8,128)(2,1)} %bitcast.19, bf16[512,3072]{1,0:T(8,128)(2,1)S(1)} %copy-done), kind=kOutput, calls=%fused_computation | convolution fusion | flops 403046400 | bytes 4063232 | tf_op jit(solution)/shard_map/dot_general | solution.py:455
  4.9 2.3 %copy.7 = bf16[128,3072]{0,1:T(8,128)(2,1)} copy(bf16[128,3072]{1,0:T(8,128)(2,1)} %convolution_convert_fusion) | data formatting | bytes 1572864 | tf_op jit(solution)/shard_map/convert_element_type | solution.py:455
  7.2 2.3 %copy.12 = bf16[16,2,128,96]{3,2,1,0:T(8,128)(2,1)} copy(bf16[16,2,128,96]{2,3,1,0:T(8,128)(2,1)} %bitcast.21) | data formatting | bytes 1572864
  9.5 2.6 %pad.8.clone = bf16[16,2,128,128]{3,2,1,0:T(8,128)(2,1)} pad(bf16[16,2,128,96]{3,2,1,0:T(8,128)(2,1)} %copy.12, bf16[]{:T(256)} %constant.25.clone.1), padding=0_0x0_0x0_0x0_32 | pad | bytes 1835010 | tf_op jit(solution)/shard_map/jit(_pad)/pad | solution.py:452
  12.1 1.0 constant_dynamic-slice_fusion.2
  13.0 0.1 stack.10
  13.2 0.1 stack.9
  13.4 1.2 copy-done.1
  14.6 59.4 %gather.1 = (bf16[4,16,32,512]{3,2,1,0:T(8,128)(2,1)S(1)}, bf16[4,32,512]{2,1,0:T(8,128)(2,1)S(1)}, bf16[4,2,16,32,128]{4,3,2,1,0:T(8,128)(2,1)S(1)}, f32[2,4,32...) custom-call(bf16[4,32,512]{2,1,0:T(8,128)(2,1)S(1)} %copy-done.5, bf16[16,256,128]{2,1,0:T(8,128)(2,1)S(1)} %bitcast.17, ...), custom_call_target="tpu_custom_call" | custom-call | tf_op jit(solution)/shard_map/gather/pallas_call | solution.py:423
  74.0 1.3 copy-done.2
  75.4 71.8 %scores.1 = (bf16[4,16,32,512]{3,2,1,0:T(8,128)(2,1)S(1)}, bf16[256,4096]{1,0:T(8,128)(2,1)S(1)}) custom-call(bf16[4,16,32,512]{3,2,1,0:T(8,128)(2,1)} %copy-done.2, bf16[4,32,512]{2,1,0:T(8,128)(2,1)S(1)} %get-tuple-element.12.kpair), custom_call_target="tpu_custom_call" | custom-call | tf_op jit(solution)/shard_map/scores/pallas_call | solution.py:423
  147.2 0.0 copy-start.6
  147.2 1.3 copy-done.6
  148.5 56.7 %rounds.1 = (bf16[2,4,32,128]{3,2,1,0:T(8,128)(2,1)S(1)}, bf16[4,2,16,32,128]{4,3,2,1,0:T(8,128)(2,1)S(1)}) custom-call(bf16[256,4096]{1,0:T(8,128)(2,1)S(1)} %get-tuple-element.13.sall, f32[2,4,32,128]{3,2,1,0:T(8,128)S(1)} %get-tuple-element.14.pm, bf16[2,4,32,128]{3,2,1,0:T(8,128)(2,1)S(1)} %get-tuple-element.15.vm, ...), custom_call_target="tpu_custom_call" | custom-call | tf_op jit(solution)/shard_map/rounds/pallas_call | solution.py:423
  205.3 1.0 copy-done.4
  206.2 0.1 copy.11
  206.3 0.7 reshape.38
  207.1 1.5 constant_dynamic-slice_fusion
  208.5 0.4 copy-done.3
  209.0 0.5 fusion.2
  209.4 0.2 copy-done.7
  209.6 1.1 fusion
  (14 shorter events, 0.1 us)
Async XLA Ops:
  0.6 1.9 copy-start
  7.2 5.9 %copy-start.8 = (bf16[4,32,192]{2,1,0:T(8,128)(2,1)S(1)}, bf16[4,32,192]{2,1,0:T(8,128)(2,1)}, u32[]{:S(2)}) copy-start(bf16[4,32,192]{2,1,0:T(8,128)(2,1)} %param.5) | copy-start | bytes 147460
  9.5 3.9 %copy-start.5 = (bf16[4,32,512]{2,1,0:T(8,128)(2,1)S(1)}, bf16[4,32,512]{2,1,0:T(8,128)(2,1)}, u32[]{:S(2)}) copy-start(bf16[4,32,512]{2,1,0:T(8,128)(2,1)} %key_ref.1) | copy-start | bytes 393220
  13.4 1.2 copy-start.1
  74.0 1.3 copy-start.2
  147.2 1.3 copy-start.6
  205.3 1.0 copy-start.4
  207.1 1.9 copy-start.3
  207.1 2.5 %copy-start.7 = (bf16[4,16,32,512]{3,2,1,0:T(8,128)(2,1)S(1)}, bf16[4,16,32,512]{3,2,1,0:T(8,128)(2,1)}, u32[]{:S(2)}) copy-start(bf16[4,16,32,512]{3,2,1,0:T(8,128)(2,1)} %copy-done.6) | copy-start | bytes 6291460

commit v2 on v0

v2 whole, which is shorter than its diff:
```python
import functools
import math

import jax
import jax.numpy as jnp
from jax import lax
from jax.experimental import pallas as pl
from jax.experimental.pallas import tpu as pltpu
from jax.sharding import PartitionSpec as P

MOMENTUM = 0.9
LANES = 128
TILE = 16
F32 = jnp.float32
BF16 = jnp.bfloat16
VMEM_LIMIT = 56 * 1024 * 1024
STEPS = 4
SIDE = 4
DEPTH = 8
AREA = SIDE * SIDE
STAGES = (
    ((1, 0), (3, 3)),
    ((2, 0), (2, 1), (2, 2), (2, 3)),
    ((3, 0), (3, 1), (3, 2), (1, 1), (1, 2), (1, 3)),
    ((0, 0), (0, 1), (0, 2), (0, 3)),
)
BLOCKS = [block for stage in STAGES for block in stage]
STARTS = [sum(len(stage) for stage in STAGES[:i]) for i in range(len(STAGES))]


def momentum_sum(count):
    return (1.0 - MOMENTUM**count) / (1.0 - MOMENTUM)


class Grid:
    def __init__(self):
        tok, tp = lax.axis_index("tok"), lax.axis_index("tp")
        self.tok, self.tp = tok, tp
        self.y = lax.div(tok, 2 * SIDE)
        self.zhi = lax.rem(lax.div(tok, SIDE), 2)
        self.x = lax.rem(tok, SIDE)
        self.zlo = lax.div(tp, 2)
        self.core = lax.rem(tp, 2)
        self.a = self.y * SIDE + self.x
        self.z = self.zhi * DEPTH + self.zlo
        self.group = lax.div(self.zlo, 2)
        self.par = lax.rem(self.zlo, 2)
        self.rghi = lax.div(self.zlo, 4)
        self.rglo = lax.rem(self.group, 2)

    def tok_of(self, y, zhi, x):
        return y * (2 * SIDE) + zhi * SIDE + x

    def at_xy(self, dy, dx):
        y = lax.rem(self.y + dy + SIDE, SIDE)
        x = lax.rem(self.x + dx + SIDE, SIDE)
        return (self.tok_of(y, self.zhi, x), self.tp)

    def a_at(self, dy, dx):
        y = lax.rem(self.y + dy + SIDE, SIDE)
        x = lax.rem(self.x + dx + SIDE, SIDE)
        return y * SIDE + x

    def partner(self):
        return (self.tok_of(self.y, 1 - self.zhi, self.x), self.tp)

    def sibling(self):
        return (self.tok, self.zlo * 2 + 1 - self.core)

    def pair(self):
        return (self.tok, (self.zlo + 1 - 2 * self.par) * 2 + self.core)

    def group_at(self, d):
        return lax.rem(self.group + d + DEPTH // 2, DEPTH // 2)

    def on_line(self, d):
        return (self.tok, (self.group_at(d) * 2 + self.par) * 2 + self.core)

    def on_ring(self, d):
        z = lax.rem(self.z + d + 2 * DEPTH, 2 * DEPTH)
        zhi, zlo = lax.div(z, DEPTH), lax.rem(z, DEPTH)
        return (self.tok_of(self.y, zhi, self.x), zlo * 2 + self.core)

    def owners(self):
        core = 1 - lax.div(self.x, 2)
        return [(2 * self.tp + self.zhi, lax.rem(self.zlo + k, DEPTH) * 2 + core) for k in range(DEPTH)]

    def sources(self):
        tp, zhi = lax.div(self.tok, 2), lax.rem(self.tok, 2)
        return [
            (self.tok_of(y, zhi, (1 - self.core) * 2 + x), tp) for y in range(SIDE) for x in range(SIDE // 2)
        ]


XY = [(dy, dx) for dy in range(SIDE) for dx in range(SIDE) if (dy, dx) != (0, 0)]


def remote(src, dst, send, recv, device):
    return pltpu.make_async_remote_copy(
        src_ref=src, dst_ref=dst, send_sem=send, recv_sem=recv, device_id=device, device_id_type=pl.DeviceIdType.MESH
    )


class Wave:
    def __init__(self, grid, blocks, sems, number, first, second):
        self.first, self.second = {}, {}
        send1, recv1, send2, recv2 = [sem.at[number] for sem in sems]
        for h, s in enumerate((first, second)):
            for d in range(1, SIDE):
                mine = blocks.at[s, grid.a]
                peer = grid.at_xy(d, 0) if h == 0 else grid.at_xy(0, d)
                self.first[h, d] = remote(mine, mine, send1.at[h, d], recv1.at[h, d], peer)
            for d in range(SIDE):
                held = blocks.at[s, grid.a_at(-d, 0) if h == 0 else grid.a_at(0, -d)]
                for e in range(1, SIDE):
                    peer = grid.at_xy(0, e) if h == 0 else grid.at_xy(e, 0)
                    self.second[h, d, e] = remote(held, held, send2.at[h, d, e], recv2.at[h, d, e], peer)

    def start(self):
        for d in range(1, SIDE):
            for h in range(2):
                self.first[h, d].start()
        for e in range(1, SIDE):
            for h in range(2):
                self.second[h, 0, e].start()

    def forward(self):
        for d in range(1, SIDE):
            for h in range(2):
                self.first[h, d].wait_recv()
                for e in range(1, SIDE):
                    self.second[h, d, e].start()

    def arrived(self):
        for copy in self.second.values():
            copy.wait_recv()

    def sent(self):
        for copy in list(self.first.values()) + list(self.second.values()):
            copy.wait_send()


class LineSum:
    def __init__(self, grid, bufs, sems, ranges):
        self.grid, self.ranges = grid, ranges
        self.part, self.sib, self.stage1, self.pair, self.stage2, self.recv = bufs
        sib_s, sib_r, pair_s, pair_r, line_s, line_r = sems
        self.sib_copy, self.pair_copy, self.line_copy = [], [], []
        for i, (start, size) in enumerate(ranges):
            b = pl.ds(start, size)
            self.sib_copy.append(remote(
                self.part.at[:, :, 1 - grid.core, b], self.sib.at[:, :, b], sib_s.at[i], sib_r.at[i], grid.sibling()
            ))
            self.pair_copy.append(remote(
                self.stage1.at[:, b], self.pair.at[:, b], pair_s.at[i], pair_r.at[i], grid.pair()
            ))
            self.line_copy.append([
                remote(self.stage2.at[d, b], self.recv.at[d, b], line_s.at[i, d], line_r.at[i, d], grid.on_line(d))
                for d in range(1, DEPTH // 2)
            ])

    def begin(self, i):
        self.sib_copy[i].start()

    def to_pair(self, i):
        grid, b = self.grid, pl.ds(*self.ranges[i])
        self.sib_copy[i].wait_recv()
        other = 1 - grid.par
        own = self.part[:, other, grid.core, b].astype(F32) + self.sib[:, other, b].astype(F32)
        self.stage1[:, b] = own.astype(BF16)
        self.pair_copy[i].start()

    def chip_sum(self, group, b):
        grid = self.grid
        own = self.part[group, grid.par, grid.core, b].astype(F32) + self.sib[group, grid.par, b].astype(F32)
        return own + self.pair[group, b].astype(F32)

    def to_line(self, i):
        grid, b = self.grid, pl.ds(*self.ranges[i])
        self.pair_copy[i].wait_recv()
        for d in (2, 1, 3):
            self.stage2[d, b] = self.chip_sum(grid.group_at(d), b).astype(BF16)
            self.line_copy[i][d - 1].start()

    def total(self, i):
        b = pl.ds(*self.ranges[i])
        total = self.chip_sum(self.grid.group, b)
        for d in range(1, DEPTH // 2):
            self.line_copy[i][d - 1].wait_recv()
            total = total + self.recv[d, b].astype(F32)
        return total

    def sent(self):
        for i in range(len(self.ranges)):
            self.sib_copy[i].wait_send()
            self.pair_copy[i].wait_send()
            for copy in self.line_copy[i]:
                copy.wait_send()


class RingGather:
    def __init__(self, grid, tiles, sems):
        a_s, a_r, b_s, b_r, c_s, c_r = sems
        self.strided, self.near, self.share = [], [], []
        for i, stage in enumerate(STAGES):
            b = pl.ds(STARTS[i], len(stage))
            own = tiles.at[b, grid.zhi, grid.par, grid.core, grid.rghi, grid.rglo]
            self.strided.append([
                remote(own, own, a_s.at[i, k], a_r.at[i, k], grid.on_ring(4 * k)) for k in (2, 1, 3)
            ])
            four = tiles.at[b, :, grid.par, grid.core, :, grid.rglo]
            self.near.append([
                remote(four, four, b_s.at[i, k], b_r.at[i, k], grid.on_ring(d)) for k, d in enumerate((2, 1, -1))
            ])
            all_mine = tiles.at[b, :, :, grid.core]
            self.share.append(remote(all_mine, all_mine, c_s.at[i], c_r.at[i], grid.sibling()))

    def begin(self, i):
        for copy in self.strided[i]:
            copy.start()

    def to_near(self, i):
        for copy in self.strided[i]:
            copy.wait_recv()
        for copy in self.near[i]:
            copy.start()

    def to_sibling(self, i):
        for copy in self.near[i]:
            copy.wait_recv()
        self.share[i].start()

    def arrived(self, i):
        self.share[i].wait_recv()

    def sent(self):
        for i in range(len(STAGES)):
            for copy in self.strided[i] + self.near[i]:
                copy.wait_send()
            self.share[i].wait_send()


def kernel(scale, cols, *refs):
    (
        key_ref, val_ref, cot_hbm, w_hbm, out_ref, grad_ref,
        w_ref, cot_ref, kmine, kother, kpair, vc, vc_in, call, pm, vm, ptotal,
        p0, p1, p2, p3, p4, p5, s0, s1, s2, s3, s4, s5, tiles, rall, dall, acc_f, acc_o, acc_b, comb, csend, osend, half,
        load_sem, swap_sem, wave0, wave1, wave2, wave3, c_send, c_recv,
        ps0, ps1, ps2, ps3, ps4, ps5, ss0, ss1, ss2, ss3, ss4, ss5, gs0, gs1, gs2, gs3, gs4, gs5,
        x_send, x_recv, f_send, f_recv, h_send, h_recv, o_send, o_recv,
    ) = refs
    grid = Grid()
    zhi, core, a = grid.zhi, grid.core, grid.a
    mb, width = key_ref.shape[1], key_ref.shape[2]
    rows = STEPS * mb

    loads = [pltpu.make_async_copy(w_hbm, w_ref, load_sem.at[0]), pltpu.make_async_copy(cot_hbm, cot_ref, load_sem.at[1])]
    for copy in loads:
        copy.start()
    targets = [grid.at_xy(*d) for d in XY] + [grid.sibling(), grid.pair()]
    targets += [grid.on_line(d) for d in range(1, DEPTH // 2)] + [grid.on_ring(d) for d in (4, 8, 12, 1, -1, -2)]
    targets += grid.sources()
    barrier = pltpu.get_barrier_semaphore()
    for device in targets:
        pl.semaphore_signal(barrier, inc=1, device_id=device, device_id_type=pl.DeviceIdType.MESH)

    kmine[:, a] = key_ref[...]
    key_rows = key_ref[...].reshape(rows, width)

    def padded(array):
        return jnp.concatenate([array, jnp.zeros(array.shape[:-1] + (LANES - cols,), array.dtype)], axis=-1)

    loads[0].wait()
    for zlo in range(DEPTH):
        block = jnp.dot(
            key_rows, w_ref[:, zlo * 4 * cols:(zlo + 1) * 4 * cols], preferred_element_type=F32
        )
        for c in range(2):
            for h in range(2):
                piece = padded(block[:, (2 * c + h) * cols:(2 * c + h + 1) * cols].astype(BF16))
                p0[zlo // 2, zlo % 2, c, pl.ds(h * (rows // TILE), rows // TILE)] = piece.reshape(-1, TILE, LANES)
    loads[1].wait()
    window = cot_ref[:, :, pl.ds(pl.multiple_of(grid.zlo * (4 * cols), LANES), 4 * cols)]
    window = jnp.where(core == 0, window[:, :, :2 * cols], window[:, :, 2 * cols:])
    for h in range(2):
        vc[h, 0] = padded(val_ref[:, :, h * cols:(h + 1) * cols])
        vc[h, 1] = padded(window[:, :, h * cols:(h + 1) * cols])
    pl.semaphore_wait(barrier, len(targets))

    def key_swap(s):
        return remote(key_ref.at[s], kpair.at[s], swap_sem.at[0, s], swap_sem.at[1, s], grid.partner())

    waves = (wave0, wave1, wave2, wave3)
    early = Wave(grid, kmine, waves, 0, 0, 3)
    late = Wave(grid, kmine, waves, 1, 1, 2)
    across = [Wave(grid, kother, waves, 2, 0, 3), Wave(grid, kother, waves, 3, 1, 2)]
    key_swaps = [key_swap(s) for s in range(STEPS)]
    vc_swap = remote(vc.at[1 - zhi], vc_in, swap_sem.at[0, STEPS], swap_sem.at[1, STEPS], grid.partner())
    psum = LineSum(grid, (p0, p1, p2, p3, p4, p5), (ps0, ps1, ps2, ps3, ps4, ps5), [(0, 2 * rows // TILE)])
    scores = LineSum(
        grid, (s0, s1, s2, s3, s4, s5), (ss0, ss1, ss2, ss3, ss4, ss5), [(STARTS[i], len(STAGES[i])) for i in range(4)]
    )
    ring = RingGather(grid, tiles, (gs0, gs1, gs2, gs3, gs4, gs5))

    early.start()
    key_swaps[3].start()
    key_swaps[1].start()
    psum.begin(0)
    psum.to_pair(0)
    early.forward()
    late.start()
    key_swaps[0].start()
    key_swaps[2].start()
    vc_swap.start()
    psum.to_line(0)

    def partial(stage):
        for t, s in STAGES[stage]:
            b = BLOCKS.index((t, s))
            left = jnp.concatenate(
                [jnp.where(zhi == 0, key_ref[t], kpair[t]), jnp.where(zhi == 0, kpair[t], key_ref[t])], axis=0
            )
            right = kmine[s].reshape(AREA * mb, width)
            block = lax.dot_general(left, right, (((1,), (1,)), ((), ())), preferred_element_type=F32).astype(BF16)
            for group in range(4):
                for q in range(4):
                    s0[group, q // 2, q % 2, b] = block[group * TILE:(group + 1) * TILE, q * LANES:(q + 1) * LANES]
        scores.begin(stage)

    def summed(stage):
        b = pl.ds(STARTS[stage], len(STAGES[stage]))
        tiles[b, zhi, grid.par, core, grid.rghi, grid.rglo] = scores.total(stage).astype(BF16)
        ring.begin(stage)

    def exchange(store, index, number, value):
        store[index, :, a] = value
        mine = store.at[index, :, a]
        copies = [
            remote(mine, mine, x_send.at[number, dy, dx], x_recv.at[number, dy, dx], grid.at_xy(dy, dx)) for dy, dx in XY
        ]
        for copy in copies:
            copy.start()
        return copies

    def received(copies):
        for copy in copies:
            copy.wait_recv()

    early.arrived()
    key_swaps[3].wait_recv()
    key_swaps[1].wait_recv()
    partial(0)
    scores.to_pair(0)
    late.forward()
    vc_swap.wait_recv()
    vm[zhi] = vc[zhi, 0]
    vm[1 - zhi] = vc_in[0]
    call[:, zhi, a] = vc[zhi, 1]
    call[:, 1 - zhi, a] = vc_in[1]
    own_c = call.at[:, :, a]
    spread = [remote(own_c, own_c, c_send.at[dy, dx], c_recv.at[dy, dx], grid.at_xy(dy, dx)) for dy, dx in XY]
    for copy in spread:
        copy.start()
    scores.to_line(0)

    ptotal[...] = psum.total(0).reshape(ptotal.shape)
    pm[zhi] = ptotal[zhi]
    p_swap = remote(ptotal.at[1 - zhi], pm.at[zhi], swap_sem.at[0, STEPS + 1], swap_sem.at[1, STEPS + 1], grid.partner())
    p_swap.start()

    summed(0)
    late.arrived()
    key_swaps[0].wait_recv()
    key_swaps[2].wait_recv()
    kother[:, a] = kpair[...]
    partial(1)
    scores.to_pair(1)
    partial(2)
    partial(3)
    ring.to_near(0)
    for wave in across:
        wave.start()
    scores.to_pair(2)
    scores.to_pair(3)
    scores.to_line(1)
    p_swap.wait_recv()

    acc_f[...] = jnp.zeros_like(acc_f)
    acc_o[...] = jnp.zeros_like(acc_o)
    acc_b[...] = jnp.zeros_like(acc_b)

    def tile_rows(t, s):
        b = BLOCKS.index((t, s))
        return jnp.concatenate(
            [tiles[b, h, p, c].reshape(4 * TILE, LANES) for h in range(2) for p in range(2) for c in range(2)], axis=1
        )

    def product(t, s, right):
        return jnp.dot(tile_rows(t, s), right.reshape(2 * AREA * mb, LANES), preferred_element_type=F32)

    def add_residual(t, s):
        term = product(t, s, rall[s])
        if t > s:
            acc_f[t] += (scale * momentum_sum(t - s)) * term
        acc_o[t] += (scale * momentum_sum(t + 1 - s)) * term

    def add_cotangent(s, t):
        acc_b[s] += (scale * momentum_sum(t + 1 - s)) * product(s, t, call[t])

    def add_adjoint(s, t):
        acc_b[s] += (scale * momentum_sum(t - s)) * product(s, t, dall[t])

    def projected(t):
        return pm[:, t].reshape(2 * mb, LANES)

    def residual(t):
        value = (projected(t) - acc_f[t] - vm[:, t].reshape(2 * mb, LANES).astype(F32)).astype(BF16)
        return exchange(rall, t, t, value.reshape(2, mb, LANES))

    def adjoint(s):
        value = (-acc_b[s]).astype(BF16).reshape(2, mb, LANES)
        copies = exchange(dall, s, STEPS + s, value) if s else []
        total = (value.astype(F32) + call[s, :, a].astype(F32)).astype(BF16)
        csend[s] = total
        x_hi, x_lo = lax.div(grid.x, 2), lax.rem(grid.x, 2)
        far = [
            remote(
                csend.at[s], comb.at[s, :, grid.y, x_hi, x_lo], f_send.at[s, k], f_recv.at[s, grid.y, x_lo], device
            )
            for k, device in enumerate(grid.owners())
        ]
        for copy in far:
            copy.start()
        return copies, far

    def gathered(s, far):
        for y in range(SIDE):
            for x in range(SIDE // 2):
                slot = comb.at[s, :, y, 1 - core, x]
                remote(csend.at[s], slot, f_send.at[s, 0], f_recv.at[s, y, x], grid.owners()[0]).wait_recv()
        held = comb.at[s, :, :, 1 - core]
        copy = remote(held, held, h_send.at[s], h_recv.at[s], grid.sibling())
        copy.start()
        return copy

    def gradient(s):
        total = None
        for blocks, which in ((kmine, zhi), (kother, 1 - zhi)):
            term = lax.dot_general(
                comb[s, which].reshape(AREA * mb, LANES), blocks[s].reshape(AREA * mb, width),
                (((0,), (0,)), ((), ())), preferred_element_type=F32,
            )
            total = term if total is None else total + term
        return total

    def output(t):
        osend[:, t] = (projected(t) - acc_o[t]).astype(BF16).reshape(2, mb, LANES)
        half[zhi, t] = osend[zhi, t]
        copy = remote(osend.at[1 - zhi, t], half.at[zhi, t], o_send.at[t], o_recv.at[t], grid.partner())
        copy.start()
        return copy

    r_copies, d_copies, far, shared, given = {}, {}, {}, {}, {}
    r_copies[0] = residual(0)
    scores.to_line(2)
    scores.to_line(3)
    ring.to_sibling(0)
    received(spread)
    summed(1)
    ring.arrived(0)

    add_cotangent(3, 3)
    d_copies[3], far[3] = adjoint(3)
    received(r_copies[0])
    add_residual(1, 0)
    r_copies[1] = residual(1)
    summed(2)
    for wave in across:
        wave.forward()
    ring.to_near(1)
    summed(3)
    ring.to_near(2)
    ring.to_sibling(1)
    ring.to_near(3)
    ring.arrived(1)
    add_cotangent(2, 2)
    add_cotangent(2, 3)
    add_residual(2, 0)

    received(d_copies[3])
    add_adjoint(2, 3)
    d_copies[2], far[2] = adjoint(2)
    received(r_copies[1])
    add_residual(2, 1)
    r_copies[2] = residual(2)
    ring.to_sibling(2)
    ring.arrived(2)
    for t in (1, 2, 3):
        add_cotangent(1, t)
    add_adjoint(1, 3)
    add_residual(3, 0)
    add_residual(3, 1)

    received(d_copies[2])
    add_adjoint(1, 2)
    d_copies[1], far[1] = adjoint(1)
    received(r_copies[2])
    add_residual(3, 2)
    r_copies[3] = residual(3)
    ring.to_sibling(3)
    ring.arrived(3)
    for t in range(STEPS):
        add_cotangent(0, t)
    add_adjoint(0, 3)
    add_adjoint(0, 2)

    received(d_copies[1])
    add_adjoint(0, 1)
    _, far[0] = adjoint(0)
    add_residual(0, 0)
    given[0] = output(0)
    add_residual(1, 1)
    given[1] = output(1)
    add_residual(2, 2)
    given[2] = output(2)
    received(r_copies[3])
    add_residual(3, 3)
    given[3] = output(3)
    for wave in across:
        wave.arrived()
    for s in (3, 2, 1):
        shared[s] = gathered(s, far[s])
    total = None
    for s in (3, 2, 1):
        shared[s].wait_recv()
        total = gradient(s) if total is None else total + gradient(s)
    shared[0] = gathered(0, far[0])
    shared[0].wait_recv()
    total = total + gradient(0)
    grad_ref[...] = total.T[:, :cols].astype(BF16)
    for t in range(STEPS):
        given[t].wait_recv()
        out_ref[t] = jnp.concatenate([half[0, t][:, :cols], half[1, t][:, :cols]], axis=-1)

    early.sent()
    late.sent()
    for wave in across:
        wave.sent()
    psum.sent()
    scores.sent()
    ring.sent()
    for copy in key_swaps + [vc_swap, p_swap] + spread + list(given.values()) + list(shared.values()):
        copy.wait_send()
    for group in list(r_copies.values()) + list(d_copies.values()) + list(far.values()):
        for copy in group:
            copy.wait_send()


def per_device(keys, values, cotangent, init_weight):
    steps, mb, width = keys.shape
    model_width = init_weight.shape[1]
    tok_count, tp_count = lax.axis_size("tok"), lax.axis_size("tp")
    cols = model_width // (2 * tp_count)
    hidden, batch_size = width * tp_count, mb * tok_count
    inner_rate = 0.5 * batch_size / (math.sqrt(hidden) + math.sqrt(batch_size)) ** 2
    scale = inner_rate / batch_size
    dma = pltpu.SemaphoreType.DMA
    rows = steps * mb
    blocks = 2 * rows // TILE

    def sums():
        return [
            pltpu.VMEM((4, 2, 2, blocks, TILE, LANES), BF16), pltpu.VMEM((4, 2, blocks, TILE, LANES), BF16),
        ] + [pltpu.VMEM((4, blocks, TILE, LANES), BF16)] * 4

    def sum_sems(count):
        return [dma((count,))] * 4 + [dma((count, 4))] * 2

    own = (steps, 2, AREA, mb, LANES)
    half = (2, steps, mb, LANES)
    scratch = [
        pltpu.VMEM(init_weight.shape, BF16), pltpu.VMEM(cotangent.shape, BF16),
        pltpu.VMEM((steps, AREA, mb, width), BF16), pltpu.VMEM((steps, AREA, mb, width), BF16),
        pltpu.VMEM(keys.shape, BF16),
        pltpu.VMEM((2, 2, steps, mb, LANES), BF16), pltpu.VMEM((2, steps, mb, LANES), BF16),
        pltpu.VMEM(own, BF16), pltpu.VMEM(half, F32), pltpu.VMEM(half, BF16), pltpu.VMEM(half, F32),
        *sums(), *sums(),
        pltpu.VMEM((16, 2, 2, 2, 2, 2, TILE, LANES), BF16),
        pltpu.VMEM(own, BF16), pltpu.VMEM(own, BF16),
        pltpu.VMEM((steps, 2 * mb, LANES), F32), pltpu.VMEM((steps, 2 * mb, LANES), F32),
        pltpu.VMEM((steps, 2 * mb, LANES), F32),
        pltpu.VMEM((steps, 2, SIDE, 2, SIDE // 2, mb, LANES), BF16), pltpu.VMEM((steps, 2, mb, LANES), BF16),
        pltpu.VMEM(half, BF16), pltpu.VMEM(half, BF16),
        dma((2,)), dma((2, steps + 2)),
        dma((4, 2, SIDE)), dma((4, 2, SIDE)), dma((4, 2, SIDE, SIDE)), dma((4, 2, SIDE, SIDE)),
        dma((SIDE, SIDE)), dma((SIDE, SIDE)),
        *sum_sems(1), *sum_sems(4),
        dma((4, 4)), dma((4, 4)), dma((4, 3)), dma((4, 3)), dma((4,)), dma((4,)),
        dma((2 * steps, SIDE, SIDE)), dma((2 * steps, SIDE, SIDE)),
        dma((steps, DEPTH)), dma((steps, SIDE, SIDE // 2)), dma((steps,)), dma((steps,)), dma((steps,)), dma((steps,)),
    ]
    vmem, hbm = pl.BlockSpec(memory_space=pltpu.VMEM), pl.BlockSpec(memory_space=pl.ANY)
    return pl.pallas_call(
        functools.partial(kernel, scale, cols),
        name="step",
        out_shape=[
            jax.ShapeDtypeStruct((steps, mb, 2 * cols), BF16), jax.ShapeDtypeStruct((width, cols), BF16),
        ],
        in_specs=[vmem, vmem, hbm, hbm],
        out_specs=[vmem, vmem],
        scratch_shapes=scratch,
        compiler_params=pltpu.CompilerParams(collective_id=0, has_side_effects=True, vmem_limit_bytes=VMEM_LIMIT),
    )(keys, values, cotangent, init_weight)


def solution(mesh):
    return jax.shard_map(
        per_device,
        mesh=mesh,
        in_specs=(P(None, "tok", "tp"), P(None, "tok", "tp"), P(None, "tok", None), P("tp", None)),
        out_specs=(P(None, "tok", "tp"), P("tp", "tok")),
        check_vma=False,
    )
```

time: 1690 us -> 157 us (0.09)
  the two profiles are of different devices: /device:TPU:2 before, /device:TPU:26 now
where the time goes in v2:
time: 157 us
  Pallas kernels  153 us (97%)
  local copies, waits for them, and re-layouts  3.11 us (2%)
    pallas_call x1, Pallas kernels, per_device(): pl.pallas_call(functools.partial(kernel, scale, cols), name='step', out_s...  153 us

profile of v2, /device:TPU:26, one launch (start us, length us, event | category | flops | bytes accessed | tf_op | source)
XLA Modules:
  0.0 156.8 jit_solution(5068675558395163948)
XLA Ops:
  0.6 153.1 %step.1 = (bf16[4,32,192]{2,1,0:T(8,128)(2,1)}, bf16[512,96]{1,0:T(8,128)(2,1)}) custom-call(bf16[4,32,512]{2,1,0:T(8,128)(2,1)} %refs_0_.1, bf16[4,32,192]{2,1,0:T(8,128)(2,1)} %refs_1_.1, bf16[4,32,3072]{2,1,0:T(8,128)(2,1)} %refs_2_.1, bf16[512,3072]{1,0:T(8,128)(2,1)} %refs_3_.1), custom_call_target="tpu_custom_call" | custom-call | tf_op jit(solution)/shard_map/step/pallas_call | solution.py:603
  153.7 1.6 %copy.6 = bf16[512,96]{0,1:T(8,128)(2,1)} copy(bf16[512,96]{1,0:T(8,128)(2,1)} %get-tuple-element.3) | data formatting | bytes 196608 | tf_op jit(solution)/shard_map/step/pallas_call | solution.py:603
  155.4 1.5 copy.8

commit v3 on v2

--- a/solution.py
+++ b/solution.py
@@ -101,43 +101,46 @@
     )
 
 
+def await_recv(like, sem):
+    pltpu.make_async_copy(like, like, sem).wait()
+
+
 class Wave:
     def __init__(self, grid, blocks, sems, number, first, second):
-        self.first, self.second = {}, {}
-        send1, recv1, send2, recv2 = [sem.at[number] for sem in sems]
+        self.first, self.own, self.rest, self.blocks = [], [], [[], []], blocks
+        send, recv1, recv2 = [sem.at[number] for sem in sems]
+        self.send, self.recv1, self.recv2 = send, recv1, recv2
         for h, s in enumerate((first, second)):
             for d in range(1, SIDE):
                 mine = blocks.at[s, grid.a]
                 peer = grid.at_xy(d, 0) if h == 0 else grid.at_xy(0, d)
-                self.first[h, d] = remote(mine, mine, send1.at[h, d], recv1.at[h, d], peer)
+                self.first.append(remote(mine, mine, send, recv1.at[h], peer))
             for d in range(SIDE):
                 held = blocks.at[s, grid.a_at(-d, 0) if h == 0 else grid.a_at(0, -d)]
                 for e in range(1, SIDE):
                     peer = grid.at_xy(0, e) if h == 0 else grid.at_xy(e, 0)
-                    self.second[h, d, e] = remote(held, held, send2.at[h, d, e], recv2.at[h, d, e], peer)
+                    copy = remote(held, held, send, recv2, peer)
+                    (self.rest[h] if d else self.own).append(copy)
 
     def start(self):
-        for d in range(1, SIDE):
-            for h in range(2):
-                self.first[h, d].start()
-        for e in range(1, SIDE):
-            for h in range(2):
-                self.second[h, 0, e].start()
+        for copy in self.first:
+            copy.start()
+
+    def start_own(self):
+        for copy in self.own:
+            copy.start()
 
     def forward(self):
-        for d in range(1, SIDE):
-            for h in range(2):
-                self.first[h, d].wait_recv()
-                for e in range(1, SIDE):
-                    self.second[h, d, e].start()
+        for h in range(2):
+            await_recv(self.blocks.at[0, pl.ds(0, SIDE - 1)], self.recv1.at[h])
+            for copy in self.rest[h]:
+                copy.start()
 
     def arrived(self):
-        for copy in self.second.values():
-            copy.wait_recv()
+        await_recv(self.blocks.at[pl.ds(0, 2), pl.ds(0, SIDE * (SIDE - 1))], self.recv2)
 
     def sent(self):
-        for copy in list(self.first.values()) + list(self.second.values()):
-            copy.wait_send()
+        await_recv(self.blocks.at[pl.ds(0, 2), pl.ds(0, (SIDE + 1) * (SIDE - 1))], self.send)
 
 
 class LineSum:
@@ -146,6 +149,7 @@
         self.part, self.sib, self.stage1, self.pair, self.stage2, self.recv = bufs
         sib_s, sib_r, pair_s, pair_r, line_s, line_r = sems
         self.sib_copy, self.pair_copy, self.line_copy = [], [], []
+        self.line_s, self.line_r = line_s, line_r
         for i, (start, size) in enumerate(ranges):
             b = pl.ds(start, size)
             self.sib_copy.append(remote(
@@ -155,7 +159,7 @@
                 self.stage1.at[:, b], self.pair.at[:, b], pair_s.at[i], pair_r.at[i], grid.pair()
             ))
             self.line_copy.append([
-                remote(self.stage2.at[d, b], self.recv.at[d, b], line_s.at[i, d], line_r.at[i, d], grid.on_line(d))
+                remote(self.stage2.at[d, b], self.recv.at[d, b], line_s.at[i], line_r.at[i], grid.on_line(d))
                 for d in range(1, DEPTH // 2)
             ])
 
@@ -185,8 +189,8 @@
     def total(self, i):
         b = pl.ds(*self.ranges[i])
         total = self.chip_sum(self.grid.group, b)
+        await_recv(self.recv.at[pl.ds(1, DEPTH // 2 - 1), b], self.line_r.at[i])
         for d in range(1, DEPTH // 2):
-            self.line_copy[i][d - 1].wait_recv()
             total = total + self.recv[d, b].astype(F32)
         return total
 
@@ -194,40 +198,42 @@
         for i in range(len(self.ranges)):
             self.sib_copy[i].wait_send()
             self.pair_copy[i].wait_send()
-            for copy in self.line_copy[i]:
-                copy.wait_send()
+            await_recv(self.stage2.at[pl.ds(1, DEPTH // 2 - 1), pl.ds(*self.ranges[i])], self.line_s.at[i])
 
 
 class RingGather:
     def __init__(self, grid, tiles, sems):
         a_s, a_r, b_s, b_r, c_s, c_r = sems
+        self.tiles, self.sems = tiles, sems
         self.strided, self.near, self.share = [], [], []
         for i, stage in enumerate(STAGES):
             b = pl.ds(STARTS[i], len(stage))
             own = tiles.at[b, grid.zhi, grid.par, grid.core, grid.rghi, grid.rglo]
             self.strided.append([
-                remote(own, own, a_s.at[i, k], a_r.at[i, k], grid.on_ring(4 * k)) for k in (2, 1, 3)
+                remote(own, own, a_s.at[i], a_r.at[i], grid.on_ring(4 * k)) for k in (2, 1, 3)
             ])
             four = tiles.at[b, :, grid.par, grid.core, :, grid.rglo]
             self.near.append([
-                remote(four, four, b_s.at[i, k], b_r.at[i, k], grid.on_ring(d)) for k, d in enumerate((2, 1, -1))
+                remote(four, four, b_s.at[i], b_r.at[i], grid.on_ring(d)) for d in (2, 1, -1)
             ])
             all_mine = tiles.at[b, :, :, grid.core]
             self.share.append(remote(all_mine, all_mine, c_s.at[i], c_r.at[i], grid.sibling()))
 
+    def like(self, i, near):
+        count = pl.ds(0, 3 * len(STAGES[i]) // 2)
+        return self.tiles.at[count, 0, 0] if near else self.tiles.at[count, 0, 0, 0, 0]
+
     def begin(self, i):
         for copy in self.strided[i]:
             copy.start()
 
     def to_near(self, i):
-        for copy in self.strided[i]:
-            copy.wait_recv()
+        await_recv(self.like(i, False), self.sems[1].at[i])
         for copy in self.near[i]:
             copy.start()
 
     def to_sibling(self, i):
-        for copy in self.near[i]:
-            copy.wait_recv()
+        await_recv(self.like(i, True), self.sems[3].at[i])
         self.share[i].start()
 
     def arrived(self, i):
@@ -235,8 +241,8 @@
 
     def sent(self):
         for i in range(len(STAGES)):
-            for copy in self.strided[i] + self.near[i]:
-                copy.wait_send()
+            await_recv(self.like(i, False), self.sems[0].at[i])
+            await_recv(self.like(i, True), self.sems[2].at[i])
             self.share[i].wait_send()
 
 
@@ -245,7 +251,7 @@
         key_ref, val_ref, cot_hbm, w_hbm, out_ref, grad_ref,
         w_ref, cot_ref, kmine, kother, kpair, vc, vc_in, call, pm, vm, ptotal,
         p0, p1, p2, p3, p4, p5, s0, s1, s2, s3, s4, s5, tiles, rall, dall, acc_f, acc_o, acc_b, comb, csend, osend, half,
-        load_sem, swap_sem, wave0, wave1, wave2, wave3, c_send, c_recv,
+        load_sem, swap_sem, wave0, wave1, wave2, c_send, c_recv,
         ps0, ps1, ps2, ps3, ps4, ps5, ss0, ss1, ss2, ss3, ss4, ss5, gs0, gs1, gs2, gs3, gs4, gs5,
         x_send, x_recv, f_send, f_recv, h_send, h_recv, o_send, o_recv,
     ) = refs
@@ -290,7 +296,7 @@
     def key_swap(s):
         return remote(key_ref.at[s], kpair.at[s], swap_sem.at[0, s], swap_sem.at[1, s], grid.partner())
 
-    waves = (wave0, wave1, wave2, wave3)
+    waves = (wave0, wave1, wave2)
     early = Wave(grid, kmine, waves, 0, 0, 3)
     late = Wave(grid, kmine, waves, 1, 1, 2)
     across = [Wave(grid, kother, waves, 2, 0, 3), Wave(grid, kother, waves, 3, 1, 2)]
@@ -301,18 +307,6 @@
         grid, (s0, s1, s2, s3, s4, s5), (ss0, ss1, ss2, ss3, ss4, ss5), [(STARTS[i], len(STAGES[i])) for i in range(4)]
     )
     ring = RingGather(grid, tiles, (gs0, gs1, gs2, gs3, gs4, gs5))
-
-    early.start()
-    key_swaps[3].start()
-    key_swaps[1].start()
-    psum.begin(0)
-    psum.to_pair(0)
-    early.forward()
-    late.start()
-    key_swaps[0].start()
-    key_swaps[2].start()
-    vc_swap.start()
-    psum.to_line(0)
 
     def partial(stage):
         for t, s in STAGES[stage]:
@@ -336,54 +330,14 @@
         store[index, :, a] = value
         mine = store.at[index, :, a]
         copies = [
-            remote(mine, mine, x_send.at[number, dy, dx], x_recv.at[number, dy, dx], grid.at_xy(dy, dx)) for dy, dx in XY
+            remote(mine, mine, x_send.at[number], x_recv.at[number], grid.at_xy(dy, dx)) for dy, dx in XY
         ]
         for copy in copies:
             copy.start()
-        return copies
-
-    def received(copies):
-        for copy in copies:
-            copy.wait_recv()
-
-    early.arrived()
-    key_swaps[3].wait_recv()
-    key_swaps[1].wait_recv()
-    partial(0)
-    scores.to_pair(0)
-    late.forward()
-    vc_swap.wait_recv()
-    vm[zhi] = vc[zhi, 0]
-    vm[1 - zhi] = vc_in[0]
-    call[:, zhi, a] = vc[zhi, 1]
-    call[:, 1 - zhi, a] = vc_in[1]
-    own_c = call.at[:, :, a]
-    spread = [remote(own_c, own_c, c_send.at[dy, dx], c_recv.at[dy, dx], grid.at_xy(dy, dx)) for dy, dx in XY]
-    for copy in spread:
-        copy.start()
-    scores.to_line(0)
-
-    ptotal[...] = psum.total(0).reshape(ptotal.shape)
-    pm[zhi] = ptotal[zhi]
-    p_swap = remote(ptotal.at[1 - zhi], pm.at[zhi], swap_sem.at[0, STEPS + 1], swap_sem.at[1, STEPS + 1], grid.partner())
-    p_swap.start()
-
-    summed(0)
-    late.arrived()
-    key_swaps[0].wait_recv()
-    key_swaps[2].wait_recv()
-    kother[:, a] = kpair[...]
-    partial(1)
-    scores.to_pair(1)
-    partial(2)
-    partial(3)
-    ring.to_near(0)
-    for wave in across:
-        wave.start()
-    scores.to_pair(2)
-    scores.to_pair(3)
-    scores.to_line(1)
-    p_swap.wait_recv()
+        return store.at[index, :, pl.ds(0, AREA - 1)], number
+
+    def received(sent):
+        await_recv(sent[0], x_recv.at[sent[1]])
 
     acc_f[...] = jnp.zeros_like(acc_f)
     acc_o[...] = jnp.zeros_like(acc_o)
@@ -411,7 +365,7 @@
         acc_b[s] += (scale * momentum_sum(t - s)) * product(s, t, dall[t])
 
     def projected(t):
-        return pm[:, t].reshape(2 * mb, LANES)
+        return pm[:, t].reshape(2 * mb, LANES).astype(F32)
 
     def residual(t):
         value = (projected(t) - acc_f[t] - vm[:, t].reshape(2 * mb, LANES).astype(F32)).astype(BF16)
@@ -419,26 +373,23 @@
 
     def adjoint(s):
         value = (-acc_b[s]).astype(BF16).reshape(2, mb, LANES)
-        copies = exchange(dall, s, STEPS + s, value) if s else []
+        copies = exchange(dall, s, STEPS + s, value) if s else None
         total = (value.astype(F32) + call[s, :, a].astype(F32)).astype(BF16)
         csend[s] = total
         x_hi, x_lo = lax.div(grid.x, 2), lax.rem(grid.x, 2)
         far = [
             remote(
-                csend.at[s], comb.at[s, :, grid.y, x_hi, x_lo], f_send.at[s, k], f_recv.at[s, grid.y, x_lo], device
+                csend.at[s], comb.at[s, :, grid.y, x_hi, x_lo], f_send.at[s], f_recv.at[s], device
             )
-            for k, device in enumerate(grid.owners())
+            for device in grid.owners()
         ]
         for copy in far:
             copy.start()
-        return copies, far
-
-    def gathered(s, far):
-        for y in range(SIDE):
-            for x in range(SIDE // 2):
-                slot = comb.at[s, :, y, 1 - core, x]
-                remote(csend.at[s], slot, f_send.at[s, 0], f_recv.at[s, y, x], grid.owners()[0]).wait_recv()
+        return copies
+
+    def gathered(s):
         held = comb.at[s, :, :, 1 - core]
+        await_recv(held, f_recv.at[s])
         copy = remote(held, held, h_send.at[s], h_recv.at[s], grid.sibling())
         copy.start()
         return copy
@@ -460,28 +411,80 @@
         copy.start()
         return copy
 
-    r_copies, d_copies, far, shared, given = {}, {}, {}, {}, {}
+    r_copies, d_copies, shared, given = {}, {}, {}, {}
+
+    early.start()
+    key_swaps[3].start()
+    key_swaps[1].start()
+    early.start_own()
+    psum.begin(0)
+    late.start()
+    key_swaps[2].start()
+    key_swaps[0].start()
+    psum.to_pair(0)
+    early.forward()
+    late.start_own()
+    late.forward()
+    vc_swap.start()
+    early.arrived()
+    key_swaps[3].wait_recv()
+    key_swaps[1].wait_recv()
+    partial(0)
+    psum.to_line(0)
+    scores.to_pair(0)
+    late.arrived()
+    key_swaps[2].wait_recv()
+    key_swaps[0].wait_recv()
+    partial(1)
+    scores.to_line(0)
+    scores.to_pair(1)
+    partial(2)
+    partial(3)
+    vc_swap.wait_recv()
+    vm[zhi] = vc[zhi, 0]
+    vm[1 - zhi] = vc_in[0]
+    call[:, zhi, a] = vc[zhi, 1]
+    call[:, 1 - zhi, a] = vc_in[1]
+    own_c = (call.at[pl.ds(3, 1), :, a], call.at[pl.ds(0, 3), :, a])
+    spread = [
+        remote(own_c[k], own_c[k], c_send.at[k], c_recv.at[k], grid.at_xy(dy, dx)) for k in range(2) for dy, dx in XY
+    ]
+    all_c = (call.at[pl.ds(3, 1), :, pl.ds(0, AREA - 1)], call.at[pl.ds(0, 3), :, pl.ds(0, AREA - 1)])
+    for copy in spread:
+        copy.start()
+    summed(0)
+    scores.to_line(1)
+    ptotal[...] = psum.total(0).reshape(ptotal.shape).astype(BF16)
+    pm[zhi] = ptotal[zhi]
+    p_swap = remote(ptotal.at[1 - zhi], pm.at[zhi], swap_sem.at[0, STEPS + 1], swap_sem.at[1, STEPS + 1], grid.partner())
+    p_swap.start()
+    scores.to_pair(2)
+    scores.to_pair(3)
+    kother[:, a] = kpair[...]
+    ring.to_near(0)
+    for wave in across:
+        wave.start()
+        wave.start_own()
+    summed(1)
+    p_swap.wait_recv()
     r_copies[0] = residual(0)
+    ring.to_sibling(0)
     scores.to_line(2)
     scores.to_line(3)
-    ring.to_sibling(0)
-    received(spread)
-    summed(1)
+    await_recv(all_c[0], c_recv.at[0])
     ring.arrived(0)
 
     add_cotangent(3, 3)
-    d_copies[3], far[3] = adjoint(3)
+    d_copies[3] = adjoint(3)
     received(r_copies[0])
     add_residual(1, 0)
     r_copies[1] = residual(1)
+    ring.to_near(1)
     summed(2)
     for wave in across:
         wave.forward()
-    ring.to_near(1)
-    summed(3)
-    ring.to_near(2)
     ring.to_sibling(1)
-    ring.to_near(3)
+    await_recv(all_c[1], c_recv.at[1])
     ring.arrived(1)
     add_cotangent(2, 2)
     add_cotangent(2, 3)
@@ -489,10 +492,12 @@
 
     received(d_copies[3])
     add_adjoint(2, 3)
-    d_copies[2], far[2] = adjoint(2)
+    d_copies[2] = adjoint(2)
     received(r_copies[1])
     add_residual(2, 1)
     r_copies[2] = residual(2)
+    ring.to_near(2)
+    summed(3)
     ring.to_sibling(2)
     ring.arrived(2)
     for t in (1, 2, 3):
@@ -503,10 +508,11 @@
 
     received(d_copies[2])
     add_adjoint(1, 2)
-    d_copies[1], far[1] = adjoint(1)
+    d_copies[1] = adjoint(1)
     received(r_copies[2])
     add_residual(3, 2)
     r_copies[3] = residual(3)
+    ring.to_near(3)
     ring.to_sibling(3)
     ring.arrived(3)
     for t in range(STEPS):
@@ -516,7 +522,7 @@
 
     received(d_copies[1])
     add_adjoint(0, 1)
-    _, far[0] = adjoint(0)
+    adjoint(0)
     add_residual(0, 0)
     given[0] = output(0)
     add_residual(1, 1)
@@ -529,15 +535,15 @@
     for wave in across:
         wave.arrived()
     for s in (3, 2, 1):
-        shared[s] = gathered(s, far[s])
+        shared[s] = gathered(s)
     total = None
     for s in (3, 2, 1):
         shared[s].wait_recv()
         total = gradient(s) if total is None else total + gradient(s)
-    shared[0] = gathered(0, far[0])
+    shared[0] = gathered(0)
     shared[0].wait_recv()
     total = total + gradient(0)
-    grad_ref[...] = total.T[:, :cols].astype(BF16)
+    grad_ref[...] = total[:cols].astype(BF16)
     for t in range(STEPS):
         given[t].wait_recv()
         out_ref[t] = jnp.concatenate([half[0, t][:, :cols], half[1, t][:, :cols]], axis=-1)
@@ -549,11 +555,14 @@
     psum.sent()
     scores.sent()
     ring.sent()
-    for copy in key_swaps + [vc_swap, p_swap] + spread + list(given.values()) + list(shared.values()):
+    for copy in key_swaps + [vc_swap, p_swap] + list(given.values()) + list(shared.values()):
         copy.wait_send()
-    for group in list(r_copies.values()) + list(d_copies.values()) + list(far.values()):
-        for copy in group:
-            copy.wait_send()
+    for k in range(2):
+        await_recv(all_c[k], c_send.at[k])
+    for like, number in list(r_copies.values()) + list(d_copies.values()):
+        await_recv(like, x_send.at[number])
+    for s in range(STEPS):
+        await_recv(comb.at[s, :, :, 1 - core], f_send.at[s])
 
 
 def per_device(keys, values, cotangent, init_weight):
@@ -574,7 +583,7 @@
         ] + [pltpu.VMEM((4, blocks, TILE, LANES), BF16)] * 4
 
     def sum_sems(count):
-        return [dma((count,))] * 4 + [dma((count, 4))] * 2
+        return [dma((count,))] * 6
 
     own = (steps, 2, AREA, mb, LANES)
     half = (2, steps, mb, LANES)
@@ -583,7 +592,7 @@
         pltpu.VMEM((steps, AREA, mb, width), BF16), pltpu.VMEM((steps, AREA, mb, width), BF16),
         pltpu.VMEM(keys.shape, BF16),
         pltpu.VMEM((2, 2, steps, mb, LANES), BF16), pltpu.VMEM((2, steps, mb, LANES), BF16),
-        pltpu.VMEM(own, BF16), pltpu.VMEM(half, F32), pltpu.VMEM(half, BF16), pltpu.VMEM(half, F32),
+        pltpu.VMEM(own, BF16), pltpu.VMEM(half, BF16), pltpu.VMEM(half, BF16), pltpu.VMEM(half, BF16),
         *sums(), *sums(),
         pltpu.VMEM((16, 2, 2, 2, 2, 2, TILE, LANES), BF16),
         pltpu.VMEM(own, BF16), pltpu.VMEM(own, BF16),
@@ -592,25 +601,25 @@
         pltpu.VMEM((steps, 2, SIDE, 2, SIDE // 2, mb, LANES), BF16), pltpu.VMEM((steps, 2, mb, LANES), BF16),
         pltpu.VMEM(half, BF16), pltpu.VMEM(half, BF16),
         dma((2,)), dma((2, steps + 2)),
-        dma((4, 2, SIDE)), dma((4, 2, SIDE)), dma((4, 2, SIDE, SIDE)), dma((4, 2, SIDE, SIDE)),
-        dma((SIDE, SIDE)), dma((SIDE, SIDE)),
+        dma((4,)), dma((4, 2)), dma((4,)), dma((2,)), dma((2,)),
         *sum_sems(1), *sum_sems(4),
-        dma((4, 4)), dma((4, 4)), dma((4, 3)), dma((4, 3)), dma((4,)), dma((4,)),
-        dma((2 * steps, SIDE, SIDE)), dma((2 * steps, SIDE, SIDE)),
-        dma((steps, DEPTH)), dma((steps, SIDE, SIDE // 2)), dma((steps,)), dma((steps,)), dma((steps,)), dma((steps,)),
+        *[dma((4,))] * 6,
+        dma((2 * steps,)), dma((2 * steps,)),
+        *[dma((steps,))] * 6,
     ]
     vmem, hbm = pl.BlockSpec(memory_space=pltpu.VMEM), pl.BlockSpec(memory_space=pl.ANY)
-    return pl.pallas_call(
+    out, grad = pl.pallas_call(
         functools.partial(kernel, scale, cols),
         name="step",
         out_shape=[
-            jax.ShapeDtypeStruct((steps, mb, 2 * cols), BF16), jax.ShapeDtypeStruct((width, cols), BF16),
+            jax.ShapeDtypeStruct((steps, mb, 2 * cols), BF16), jax.ShapeDtypeStruct((cols, width), BF16),
         ],
         in_specs=[vmem, vmem, hbm, hbm],
         out_specs=[vmem, vmem],
         scratch_shapes=scratch,
         compiler_params=pltpu.CompilerParams(collective_id=0, has_side_effects=True, vmem_limit_bytes=VMEM_LIMIT),
     )(keys, values, cotangent, init_weight)
+    return out, grad.T
 
 
 def solution(mesh):

time: 157 us -> 145 us (0.924)
  the two profiles are of different devices: /device:TPU:26 before, /device:TPU:3 now
where the time goes in v3:
time: 145 us; the launch traced here: 144 us
  Pallas kernels  141 us (97%)
  local copies, waits for them, and re-layouts  3.01 us (2%)
    pallas_call x1, Pallas kernels, per_device(): pl.pallas_call(functools.partial(kernel, scale, cols), name='step', out_s...  141 us
    unnamed x2, local copies, waits for them, and re-layouts  3.01 us

profile of v3, /device:TPU:3, one launch (start us, length us, event | category | flops | bytes accessed | tf_op | source)
XLA Modules:
  0.0 144.3 jit_solution(6721216044775197713)
XLA Ops:
  0.6 140.7 %step.1 = (bf16[4,32,192]{2,1,0:T(8,128)(2,1)}, bf16[96,512]{1,0:T(8,128)(2,1)}) custom-call(bf16[4,32,512]{2,1,0:T(8,128)(2,1)} %refs_0_.1, bf16[4,32,192]{2,1,0:T(8,128)(2,1)} %refs_1_.1, bf16[4,32,3072]{2,1,0:T(8,128)(2,1)} %refs_2_.1, bf16[512,3072]{1,0:T(8,128)(2,1)} %refs_3_.1), custom_call_target="tpu_custom_call" | custom-call | tf_op jit(solution)/shard_map/step/pallas_call | solution.py:611
  141.3 1.5 %copy.8 = bf16[4,32,192]{2,1,0:T(8,128)(2,1)} copy(bf16[4,32,192]{2,1,0:T(8,128)(2,1)} %get-tuple-element.8) | data formatting | bytes 98304
  142.8 1.5 %copy.9 = bf16[512,96]{0,1:T(8,128)(2,1)} copy(bf16[512,96]{0,1:T(8,128)(2,1)} %bitcast.1) | data formatting | bytes 196608

commit v4 on v3

v4 whole, which is shorter than its diff:
```python
import functools
import math

import jax
import jax.numpy as jnp
from jax import lax
from jax.experimental import pallas as pl
from jax.experimental.pallas import tpu as pltpu
from jax.sharding import PartitionSpec as P

MOMENTUM = 0.9
LANES = 128
TILE = 16
F32 = jnp.float32
BF16 = jnp.bfloat16
VMEM_LIMIT = 56 * 1024 * 1024
STEPS = 4
SIDE = 4
DEPTH = 8
AREA = SIDE * SIDE
STAGES = (
    ((1, 0), (3, 3), (2, 0), (2, 1), (2, 2), (2, 3)),
    ((3, 0), (3, 1), (3, 2), (1, 1), (1, 2), (1, 3)),
    ((0, 0), (0, 1), (0, 2), (0, 3)),
)
BLOCKS = [block for stage in STAGES for block in stage]
STARTS = [sum(len(stage) for stage in STAGES[:i]) for i in range(len(STAGES))]


def momentum_sum(count):
    return (1.0 - MOMENTUM**count) / (1.0 - MOMENTUM)


class Grid:
    def __init__(self):
        tok, tp = lax.axis_index("tok"), lax.axis_index("tp")
        self.tok, self.tp = tok, tp
        self.y = lax.div(tok, 2 * SIDE)
        self.zhi = lax.rem(lax.div(tok, SIDE), 2)
        self.x = lax.rem(tok, SIDE)
        self.zlo = lax.div(tp, 2)
        self.core = lax.rem(tp, 2)
        self.a = self.y * SIDE + self.x
        self.z = self.zhi * DEPTH + self.zlo
        self.group = lax.div(self.zlo, 2)
        self.par = lax.rem(self.zlo, 2)
        self.rghi = lax.div(self.zlo, 4)
        self.rglo = lax.rem(self.group, 2)

    def tok_of(self, y, zhi, x):
        return y * (2 * SIDE) + zhi * SIDE + x

    def at_xy(self, dy, dx):
        y = lax.rem(self.y + dy + SIDE, SIDE)
        x = lax.rem(self.x + dx + SIDE, SIDE)
        return (self.tok_of(y, self.zhi, x), self.tp)

    def a_at(self, dy, dx):
        y = lax.rem(self.y + dy + SIDE, SIDE)
        x = lax.rem(self.x + dx + SIDE, SIDE)
        return y * SIDE + x

    def partner(self):
        return (self.tok_of(self.y, 1 - self.zhi, self.x), self.tp)

    def sibling(self):
        return (self.tok, self.zlo * 2 + 1 - self.core)

    def pair(self):
        return (self.tok, (self.zlo + 1 - 2 * self.par) * 2 + self.core)

    def group_at(self, d):
        return lax.rem(self.group + d + DEPTH // 2, DEPTH // 2)

    def on_line(self, d):
        return (self.tok, (self.group_at(d) * 2 + self.par) * 2 + self.core)

    def on_ring(self, d):
        z = lax.rem(self.z + d + 2 * DEPTH, 2 * DEPTH)
        zhi, zlo = lax.div(z, DEPTH), lax.rem(z, DEPTH)
        return (self.tok_of(self.y, zhi, self.x), zlo * 2 + self.core)

    def owner(self, k):
        zlo = lax.rem(self.group + k, DEPTH // 2) * 2 + lax.rem(self.x, 2)
        return (2 * self.tp + self.zhi, zlo * 2 + 1 - lax.div(self.x, 2))

    def sources(self):
        tp, zhi = lax.div(self.tok, 2), lax.rem(self.tok, 2)
        return [(self.tok_of(y, zhi, (1 - self.core) * 2 + self.par), tp) for y in range(SIDE)]


XY = [(dy, dx) for dy in range(SIDE) for dx in range(SIDE) if (dy, dx) != (0, 0)]


def remote(src, dst, send, recv, device):
    return pltpu.make_async_remote_copy(
        src_ref=src, dst_ref=dst, send_sem=send, recv_sem=recv, device_id=device, device_id_type=pl.DeviceIdType.MESH
    )


def repeat(first, stop, body):
    def step(i, carry):
        body(i)
        return carry

    lax.fori_loop(first, stop, step, 0)


def await_recv(like, sem):
    pltpu.make_async_copy(like, like, sem).wait()


class Wave:
    def __init__(self, grid, blocks, sems, number, first, second):
        self.grid, self.blocks, self.steps = grid, blocks, (first, second)
        self.send, self.recv1, self.recv2 = [sem.at[number] for sem in sems]

    def along(self, h, d):
        return (d, 0) if h == 0 else (0, d)

    def start(self):
        def body(d):
            for h in range(2):
                mine = self.blocks.at[self.steps[h], self.grid.a]
                remote(mine, mine, self.send, self.recv1.at[h], self.grid.at_xy(*self.along(h, d))).start()

        repeat(1, SIDE, body)

    def pass_on(self, h, d, e):
        held = self.blocks.at[self.steps[h], self.grid.a_at(*self.along(h, -d))]
        remote(held, held, self.send, self.recv2, self.grid.at_xy(*self.along(1 - h, e))).start()

    def start_own(self):
        def body(e):
            for h in range(2):
                self.pass_on(h, 0, e)

        repeat(1, SIDE, body)

    def forward(self):
        for h in range(2):
            await_recv(self.blocks.at[0, pl.ds(0, SIDE - 1)], self.recv1.at[h])
            count = SIDE - 1
            repeat(0, count * count, lambda k, h=h: self.pass_on(h, lax.div(k, count) + 1, lax.rem(k, count) + 1))

    def arrived(self):
        await_recv(self.blocks.at[pl.ds(0, 2), pl.ds(0, SIDE * (SIDE - 1))], self.recv2)

    def sent(self):
        await_recv(self.blocks.at[pl.ds(0, 2), pl.ds(0, (SIDE + 1) * (SIDE - 1))], self.send)


class LineSum:
    def __init__(self, grid, bufs, sems, ranges):
        self.grid, self.ranges = grid, ranges
        self.part, self.sib, self.stage1, self.pair, self.stage2, self.recv = bufs
        sib_s, sib_r, pair_s, pair_r, line_s, line_r = sems
        self.sib_copy, self.pair_copy = [], []
        self.line_s, self.line_r = line_s, line_r
        for i, (start, size) in enumerate(ranges):
            b = pl.ds(start, size)
            self.sib_copy.append(remote(
                self.part.at[:, :, 1 - grid.core, b], self.sib.at[:, :, b], sib_s.at[i], sib_r.at[i], grid.sibling()
            ))
            self.pair_copy.append(remote(
                self.stage1.at[:, b], self.pair.at[:, b], pair_s.at[i], pair_r.at[i], grid.pair()
            ))

    def begin(self, i):
        self.sib_copy[i].start()

    def to_pair(self, i):
        grid, b = self.grid, pl.ds(*self.ranges[i])
        self.sib_copy[i].wait_recv()
        other = 1 - grid.par

        def body(group):
            own = self.part[group, other, grid.core, b].astype(F32) + self.sib[group, other, b].astype(F32)
            self.stage1[group, b] = own.astype(BF16)

        repeat(0, DEPTH // 2, body)
        self.pair_copy[i].start()

    def chip_sum(self, group, b):
        grid = self.grid
        own = self.part[group, grid.par, grid.core, b].astype(F32) + self.sib[group, grid.par, b].astype(F32)
        return own + self.pair[group, b].astype(F32)

    def to_line(self, i):
        grid, b = self.grid, pl.ds(*self.ranges[i])
        self.pair_copy[i].wait_recv()

        def body(d):
            self.stage2[d, b] = self.chip_sum(grid.group_at(d), b).astype(BF16)
            remote(self.stage2.at[d, b], self.recv.at[d, b], self.line_s.at[i], self.line_r.at[i], grid.on_line(d)).start()

        repeat(1, DEPTH // 2, body)

    def total(self, i):
        b = pl.ds(*self.ranges[i])
        total = self.chip_sum(self.grid.group, b)
        await_recv(self.recv.at[pl.ds(1, DEPTH // 2 - 1), b], self.line_r.at[i])
        for d in range(1, DEPTH // 2):
            total = total + self.recv[d, b].astype(F32)
        return total

    def sent(self):
        for i in range(len(self.ranges)):
            self.sib_copy[i].wait_send()
            self.pair_copy[i].wait_send()
            await_recv(self.stage2.at[pl.ds(1, DEPTH // 2 - 1), pl.ds(*self.ranges[i])], self.line_s.at[i])


class RingGather:
    def __init__(self, grid, tiles, sems):
        a_s, a_r, b_s, b_r, c_s, c_r = sems
        self.tiles, self.sems = tiles, sems
        self.strided, self.near, self.share = [], [], []
        for i, stage in enumerate(STAGES):
            b = pl.ds(STARTS[i], len(stage))
            own = tiles.at[b, grid.zhi, grid.par, grid.core, grid.rghi, grid.rglo]
            self.strided.append([
                remote(own, own, a_s.at[i], a_r.at[i], grid.on_ring(4 * k)) for k in (2, 1, 3)
            ])
            four = tiles.at[b, :, grid.par, grid.core, :, grid.rglo]
            self.near.append([
                remote(four, four, b_s.at[i], b_r.at[i], grid.on_ring(d)) for d in (2, 1, -1)
            ])
            all_mine = tiles.at[b, :, :, grid.core]
            self.share.append(remote(all_mine, all_mine, c_s.at[i], c_r.at[i], grid.sibling()))

    def like(self, i, near):
        count = pl.ds(0, 3 * len(STAGES[i]) // 2)
        return self.tiles.at[count, 0, 0] if near else self.tiles.at[count, 0, 0, 0, 0]

    def begin(self, i):
        for copy in self.strided[i]:
            copy.start()

    def to_near(self, i):
        await_recv(self.like(i, False), self.sems[1].at[i])
        for copy in self.near[i]:
            copy.start()

    def to_sibling(self, i):
        await_recv(self.like(i, True), self.sems[3].at[i])
        self.share[i].start()

    def arrived(self, i):
        self.share[i].wait_recv()

    def sent(self):
        for i in range(len(STAGES)):
            await_recv(self.like(i, False), self.sems[0].at[i])
            await_recv(self.like(i, True), self.sems[2].at[i])
            self.share[i].wait_send()


def kernel(scale, cols, *refs):
    (
        key_ref, val_ref, cot_hbm, w_hbm, out_ref, grad_ref,
        w_ref, cot_ref, kall, kpair, left_ref, vc, vc_in, call, pm, vm, ptotal,
        p0, p1, p2, p3, p4, p5, s0, s1, s2, s3, s4, s5, tiles, rall, dall, acc_f, acc_o, acc_b, acc_g, comb, csend, osend, half,
        load_sem, swap_sem, wave0, wave1, wave2, c_send, c_recv,
        ps0, ps1, ps2, ps3, ps4, ps5, ss0, ss1, ss2, ss3, ss4, ss5, gs0, gs1, gs2, gs3, gs4, gs5,
        x_send, x_recv, f_send, f_recv, h_send, h_recv, o_send, o_recv, q_send, q_recv,
    ) = refs
    grid = Grid()
    zhi, core, a = grid.zhi, grid.core, grid.a
    mb, width = key_ref.shape[1], key_ref.shape[2]
    kmine, kother = kall.at[0], kall.at[1]
    rows = STEPS * mb

    loads = [pltpu.make_async_copy(w_hbm, w_ref, load_sem.at[0]), pltpu.make_async_copy(cot_hbm, cot_ref, load_sem.at[1])]
    for copy in loads:
        copy.start()
    targets = [grid.at_xy(*d) for d in XY] + [grid.sibling(), grid.pair()]
    targets += [grid.on_line(d) for d in range(1, DEPTH // 2)] + [grid.on_ring(d) for d in (4, 8, 12, 1, -1, -2)]
    targets += grid.sources()
    barrier = pltpu.get_barrier_semaphore()
    for device in targets:
        pl.semaphore_signal(barrier, inc=1, device_id=device, device_id_type=pl.DeviceIdType.MESH)

    kmine[:, a] = key_ref[...]
    key_rows = key_ref[...].reshape(rows, width)

    def padded(array):
        return jnp.concatenate([array, jnp.zeros(array.shape[:-1] + (LANES - cols,), array.dtype)], axis=-1)

    loads[0].wait()

    def project(zlo):
        columns = pl.ds(pl.multiple_of(zlo * (4 * cols), LANES), 4 * cols)
        block = jnp.dot(key_rows, w_ref[:, columns], preferred_element_type=F32)
        for c in range(2):
            for h in range(2):
                piece = padded(block[:, (2 * c + h) * cols:(2 * c + h + 1) * cols].astype(BF16))
                piece = piece.reshape(STEPS, mb // TILE, TILE, LANES)
                for t in range(STEPS):
                    p0[lax.div(zlo, 2), lax.rem(zlo, 2), c, pl.ds((2 * t + h) * (mb // TILE), mb // TILE)] = piece[t]

    repeat(0, DEPTH, project)
    loads[1].wait()
    window = cot_ref[:, :, pl.ds(pl.multiple_of(grid.zlo * (4 * cols), LANES), 4 * cols)]
    window = jnp.where(core == 0, window[:, :, :2 * cols], window[:, :, 2 * cols:])
    for h in range(2):
        vc[h, 0] = padded(val_ref[:, :, h * cols:(h + 1) * cols])
        vc[h, 1] = padded(window[:, :, h * cols:(h + 1) * cols])
    pl.semaphore_wait(barrier, len(targets))

    def key_swap(s):
        return remote(key_ref.at[s], kpair.at[s], swap_sem.at[0, s], swap_sem.at[1, s], grid.partner())

    waves = (wave0, wave1, wave2)
    early = Wave(grid, kmine, waves, 0, 0, 3)
    late = Wave(grid, kmine, waves, 1, 1, 2)
    across = [Wave(grid, kother, waves, 2, 0, 3), Wave(grid, kother, waves, 3, 1, 2)]
    key_swaps = [key_swap(s) for s in range(STEPS)]

    def vc_swap(number, which, t, count):
        part = pl.ds(t, count)
        return remote(
            vc.at[1 - zhi, which, part], vc_in.at[which, part], swap_sem.at[0, number], swap_sem.at[1, number],
            grid.partner(),
        )

    vc_swaps = [vc_swap(4, 0, 0, 1), vc_swap(5, 1, 3, 1), vc_swap(6, 0, 1, 3), vc_swap(7, 1, 0, 3)]
    first = 2 * mb // TILE
    p_swap = remote(ptotal.at[1 - zhi], pm.at[zhi], swap_sem.at[0, 8], swap_sem.at[1, 8], grid.partner())
    psum = LineSum(grid, (p0, p1, p2, p3, p4, p5), (ps0, ps1, ps2, ps3, ps4, ps5), [(0, STEPS * first)])
    scores = LineSum(
        grid, (s0, s1, s2, s3, s4, s5), (ss0, ss1, ss2, ss3, ss4, ss5), [(0, STARTS[1]), (STARTS[1], len(BLOCKS) - STARTS[1])]
    )
    ring = RingGather(grid, tiles, (gs0, gs1, gs2, gs3, gs4, gs5))

    def partial(s):
        right = kmine[s].reshape(AREA * mb, width)
        block = lax.dot_general(left_ref[...], right, (((1,), (1,)), ((), ())), preferred_element_type=F32).astype(BF16)
        for t in range(STEPS):
            b = BLOCKS.index((t, s))
            for group in range(4):
                for q in range(4):
                    row = (4 * t + group) * TILE
                    s0[group, q // 2, q % 2, b] = block[row:row + TILE, q * LANES:(q + 1) * LANES]

    def summed(i):
        b = pl.ds(*scores.ranges[i])
        tiles[b, zhi, grid.par, core, grid.rghi, grid.rglo] = scores.total(i).astype(BF16)

    def to_xy(mine, send, recv):
        def body(k):
            remote(mine, mine, send, recv, grid.at_xy(lax.div(k, SIDE), lax.rem(k, SIDE))).start()

        repeat(1, AREA, body)

    def exchange(store, index, number, value):
        store[index, :, a] = value
        to_xy(store.at[index, :, a], x_send.at[number], x_recv.at[number])
        return store.at[index, :, pl.ds(0, AREA - 1)], number

    def received(sent):
        await_recv(sent[0], x_recv.at[sent[1]])

    acc_f[...] = jnp.zeros_like(acc_f)
    acc_o[...] = jnp.zeros_like(acc_o)
    acc_b[...] = jnp.zeros_like(acc_b)

    def product(b, right):
        left = jnp.concatenate(
            [tiles[b, h, p, c].reshape(4 * TILE, LANES) for h in range(2) for p in range(2) for c in range(2)], axis=1
        )
        return jnp.dot(left, right.reshape(2 * AREA * mb, LANES), preferred_element_type=F32)

    def add_residual(t, s):
        term = product(BLOCKS.index((t, s)), rall[s])
        if t > s:
            acc_f[t] += (scale * momentum_sum(t - s)) * term
        acc_o[t] += (scale * momentum_sum(t + 1 - s)) * term

    def add_adjoint(s, t):
        acc_b[s] += (scale * momentum_sum(t - s)) * product(BLOCKS.index((s, t)), dall[t])

    def add_run(s, first, stop, store, later):
        base = BLOCKS.index((s, first)) - first

        def step(t, carry):
            factor, total = carry
            total = total + factor * product(base + t, store[t])
            return scale + MOMENTUM * factor, total

        factor = jnp.float32(scale * momentum_sum(first + later - s))
        acc_b[s] += lax.fori_loop(first, stop, step, (factor, jnp.zeros((2 * mb, LANES), F32)))[1]

    def projected(t):
        return pm[:, t].reshape(2 * mb, LANES).astype(F32)

    def residual(t):
        value = (projected(t) - acc_f[t] - vm[:, t].reshape(2 * mb, LANES).astype(F32)).astype(BF16)
        return exchange(rall, t, t, value.reshape(2, mb, LANES))

    def adjoint(s):
        value = (-acc_b[s]).astype(BF16).reshape(2, mb, LANES)
        copies = exchange(dall, s, STEPS + s, value) if s else None
        total = (value.astype(F32) + call[s, :, a].astype(F32)).astype(BF16)
        csend[s] = total
        x_hi, x_lo = lax.div(grid.x, 2), lax.rem(grid.x, 2)
        slot = comb.at[s, :, grid.y, x_hi, x_lo]

        def body(k):
            remote(csend.at[s], slot, f_send.at[s], f_recv.at[s], grid.owner(k)).start()

        repeat(0, DEPTH // 2, body)
        return copies

    def to_pair(s):
        held = comb.at[s, :, :, 1 - core, grid.par]
        await_recv(held, f_recv.at[s])
        passed[s] = remote(held, held, q_send.at[s], q_recv.at[s], grid.pair())
        passed[s].start()

    def to_core(s):
        passed[s].wait_recv()
        held = comb.at[s, :, :, 1 - core]
        shared[s] = remote(held, held, h_send.at[s], h_recv.at[s], grid.sibling())
        shared[s].start()

    def gradient(s):
        def body(h):
            which = h + zhi - 2 * h * zhi
            acc_g[...] += lax.dot_general(
                comb[s, which].reshape(AREA * mb, LANES), kall[h, s].reshape(AREA * mb, width),
                (((0,), (0,)), ((), ())), preferred_element_type=F32,
            )

        repeat(0, 2, body)

    def output(t):
        osend[:, t] = (projected(t) - acc_o[t]).astype(BF16).reshape(2, mb, LANES)
        half[zhi, t] = osend[zhi, t]
        copy = remote(osend.at[1 - zhi, t], half.at[zhi, t], o_send.at[t], o_recv.at[t], grid.partner())
        copy.start()
        return copy

    r_copies, d_copies, passed, shared, given = {}, {}, {}, {}, {}

    early.start()
    key_swaps[3].start()
    key_swaps[1].start()
    psum.begin(0)
    early.start_own()
    late.start()
    key_swaps[2].start()
    key_swaps[0].start()
    psum.to_pair(0)
    early.forward()
    late.start_own()
    late.forward()
    psum.to_line(0)
    for copy in vc_swaps:
        copy.start()
    early.arrived()
    late.arrived()
    for copy in key_swaps:
        copy.wait_recv()

    for t in range(STEPS):
        near, other = key_ref[t], kpair[t]
        left_ref[pl.ds(2 * t * mb, mb)] = jnp.where(zhi == 0, near, other)
        left_ref[pl.ds((2 * t + 1) * mb, mb)] = jnp.where(zhi == 0, other, near)
    for s in range(STEPS):
        partial(s)
    scores.begin(0)
    scores.begin(1)
    scores.to_pair(0)

    ptotal[...] = psum.total(0).reshape(STEPS, 2, mb, LANES).astype(BF16).transpose(1, 0, 2, 3)
    p_swap.start()
    pm[zhi] = ptotal[zhi]
    scores.to_line(0)
    for copy in vc_swaps:
        copy.wait_recv()

    def spread(number, t, count):
        part = pl.ds(t, count)
        call[part, zhi, a] = vc[zhi, 1, part]
        call[part, 1 - zhi, a] = vc_in[1, part]
        to_xy(call.at[part, :, a], c_send.at[number], c_recv.at[number])
        return call.at[part, :, pl.ds(0, AREA - 1)]

    vm[zhi] = vc[zhi, 0]
    vm[1 - zhi] = vc_in[0]
    all_c = [spread(0, 3, 1), spread(1, 0, 3)]
    scores.to_pair(1)
    summed(0)
    ring.begin(0)
    p_swap.wait_recv()
    r_copies[0] = residual(0)
    scores.to_line(1)
    kother[:, a] = kpair[...]
    ring.to_near(0)
    for wave in across:
        wave.start()
        wave.start_own()
    ring.to_sibling(0)
    for k in range(2):
        await_recv(all_c[k], c_recv.at[k])
    ring.arrived(0)

    add_run(3, 3, 4, call, 1)
    d_copies[3] = adjoint(3)
    received(r_copies[0])
    add_residual(1, 0)
    r_copies[1] = residual(1)
    summed(1)
    ring.begin(1)
    ring.begin(2)
    add_run(2, 2, 4, call, 1)
    add_residual(2, 0)

    received(d_copies[3])
    add_adjoint(2, 3)
    d_copies[2] = adjoint(2)
    received(r_copies[1])
    add_residual(2, 1)
    r_copies[2] = residual(2)
    ring.to_near(1)
    ring.to_near(2)
    for wave in across:
        wave.forward()
    to_pair(3)
    ring.to_sibling(1)
    ring.arrived(1)
    add_run(1, 1, 4, call, 1)
    add_adjoint(1, 3)
    add_residual(3, 0)
    add_residual(3, 1)

    received(d_copies[2])
    add_adjoint(1, 2)
    d_copies[1] = adjoint(1)
    received(r_copies[2])
    add_residual(3, 2)
    r_copies[3] = residual(3)
    ring.to_sibling(2)
    ring.arrived(2)
    to_core(3)
    to_pair(2)
    add_run(0, 0, 4, call, 1)
    add_run(0, 2, 4, dall, 0)

    received(d_copies[1])
    add_adjoint(0, 1)
    adjoint(0)
    for t in range(3):
        add_residual(t, t)
        given[t] = output(t)
    received(r_copies[3])
    add_residual(3, 3)
    given[3] = output(3)
    to_core(2)
    to_pair(1)
    for wave in across:
        wave.arrived()
    acc_g[...] = jnp.zeros_like(acc_g)
    shared[3].wait_recv()
    gradient(3)
    to_core(1)
    shared[2].wait_recv()
    gradient(2)
    shared[1].wait_recv()
    gradient(1)
    to_pair(0)
    to_core(0)
    for t in range(STEPS):
        given[t].wait_recv()
        out_ref[t] = jnp.concatenate([half[0, t][:, :cols], half[1, t][:, :cols]], axis=-1)
    shared[0].wait_recv()
    gradient(0)
    grad_ref[...] = acc_g[:cols].astype(BF16)

    early.sent()
    late.sent()
    for wave in across:
        wave.sent()
    psum.sent()
    scores.sent()
    ring.sent()
    for copy in key_swaps + vc_swaps + [p_swap] + list(given.values()) + list(passed.values()) + list(shared.values()):
        copy.wait_send()
    for k in range(2):
        await_recv(all_c[k], c_send.at[k])
    for like, number in list(r_copies.values()) + list(d_copies.values()):
        await_recv(like, x_send.at[number])
    for s in range(STEPS):
        await_recv(comb.at[s, :, :, 1 - core, grid.par], f_send.at[s])


def per_device(keys, values, cotangent, init_weight):
    steps, mb, width = keys.shape
    model_width = init_weight.shape[1]
    tok_count, tp_count = lax.axis_size("tok"), lax.axis_size("tp")
    cols = model_width // (2 * tp_count)
    hidden, batch_size = width * tp_count, mb * tok_count
    inner_rate = 0.5 * batch_size / (math.sqrt(hidden) + math.sqrt(batch_size)) ** 2
    scale = inner_rate / batch_size
    dma = pltpu.SemaphoreType.DMA
    rows = steps * mb
    blocks = 2 * rows // TILE

    def sums():
        return [
            pltpu.VMEM((4, 2, 2, blocks, TILE, LANES), BF16), pltpu.VMEM((4, 2, blocks, TILE, LANES), BF16),
        ] + [pltpu.VMEM((4, blocks, TILE, LANES), BF16)] * 4

    def sum_sems(count):
        return [dma((count,))] * 6

    own = (steps, 2, AREA, mb, LANES)
    half = (2, steps, mb, LANES)
    scratch = [
        pltpu.VMEM(init_weight.shape, BF16), pltpu.VMEM(cotangent.shape, BF16),
        pltpu.VMEM((2, steps, AREA, mb, width), BF16),
        pltpu.VMEM(keys.shape, BF16), pltpu.VMEM((2 * rows, width), BF16),
        pltpu.VMEM((2, 2, steps, mb, LANES), BF16), pltpu.VMEM((2, steps, mb, LANES), BF16),
        pltpu.VMEM(own, BF16), pltpu.VMEM(half, BF16), pltpu.VMEM(half, BF16), pltpu.VMEM(half, BF16),
        *sums(), *sums(),
        pltpu.VMEM((16, 2, 2, 2, 2, 2, TILE, LANES), BF16),
        pltpu.VMEM(own, BF16), pltpu.VMEM(own, BF16),
        pltpu.VMEM((steps, 2 * mb, LANES), F32), pltpu.VMEM((steps, 2 * mb, LANES), F32),
        pltpu.VMEM((steps, 2 * mb, LANES), F32), pltpu.VMEM((LANES, width), F32),
        pltpu.VMEM((steps, 2, SIDE, 2, SIDE // 2, mb, LANES), BF16), pltpu.VMEM((steps, 2, mb, LANES), BF16),
        pltpu.VMEM(half, BF16), pltpu.VMEM(half, BF16),
        dma((2,)), dma((2, steps + 6)),
        dma((4,)), dma((4, 2)), dma((4,)), dma((2,)), dma((2,)),
        *sum_sems(1), *sum_sems(2),
        *[dma((len(STAGES),))] * 6,
        dma((2 * steps,)), dma((2 * steps,)),
        *[dma((steps,))] * 8,
    ]
    vmem, hbm = pl.BlockSpec(memory_space=pltpu.VMEM), pl.BlockSpec(memory_space=pl.ANY)
    out, grad = pl.pallas_call(
        functools.partial(kernel, scale, cols),
        name="step",
        out_shape=[
            jax.ShapeDtypeStruct((steps, mb, 2 * cols), BF16), jax.ShapeDtypeStruct((cols, width), BF16),
        ],
        in_specs=[vmem, vmem, hbm, hbm],
        out_specs=[vmem, vmem],
        scratch_shapes=scratch,
        compiler_params=pltpu.CompilerParams(collective_id=0, has_side_effects=True, vmem_limit_bytes=VMEM_LIMIT),
    )(keys, values, cotangent, init_weight)
    return out, grad.T


def solution(mesh):
    return jax.shard_map(
        per_device,
        mesh=mesh,
        in_specs=(P(None, "tok", "tp"), P(None, "tok", "tp"), P(None, "tok", None), P("tp", None)),
        out_specs=(P(None, "tok", "tp"), P("tp", "tok")),
        check_vma=False,
    )
```

time: 145 us -> 141 us (0.972)
  the two profiles are of different devices: /device:TPU:3 before, /device:TPU:1 now
where the time goes in v4:
time: 141 us
  Pallas kernels  137 us (97%)
  local copies, waits for them, and re-layouts  3.01 us (2%)
    pallas_call x1, Pallas kernels, per_device(): pl.pallas_call(functools.partial(kernel, scale, cols), name='step', out_s...  137 us
    unnamed x2, local copies, waits for them, and re-layouts  3.01 us

profile of v4, /device:TPU:1, one launch (start us, length us, event | category | flops | bytes accessed | tf_op | source)
XLA Modules:
  0.0 140.6 jit_solution(13491931983476816788)
XLA Ops:
  0.6 137.0 %step.1 = (bf16[4,32,192]{2,1,0:T(8,128)(2,1)}, bf16[96,512]{1,0:T(8,128)(2,1)}) custom-call(bf16[4,32,512]{2,1,0:T(8,128)(2,1)} %refs_0_.1, bf16[4,32,192]{2,1,0:T(8,128)(2,1)} %refs_1_.1, bf16[4,32,3072]{2,1,0:T(8,128)(2,1)} %refs_2_.1, bf16[512,3072]{1,0:T(8,128)(2,1)} %refs_3_.1), custom_call_target="tpu_custom_call" | custom-call | tf_op jit(solution)/shard_map/step/pallas_call | solution.py:641
  137.6 1.5 %copy.8 = bf16[4,32,192]{2,1,0:T(8,128)(2,1)} copy(bf16[4,32,192]{2,1,0:T(8,128)(2,1)} %get-tuple-element.8) | data formatting | bytes 98304
  139.1 1.5 %copy.9 = bf16[512,96]{0,1:T(8,128)(2,1)} copy(bf16[512,96]{0,1:T(8,128)(2,1)} %bitcast.1) | data formatting | bytes 196608

commit v5 on v4

--- a/solution.py
+++ b/solution.py
@@ -84,10 +84,6 @@
         zlo = lax.rem(self.group + k, DEPTH // 2) * 2 + lax.rem(self.x, 2)
         return (2 * self.tp + self.zhi, zlo * 2 + 1 - lax.div(self.x, 2))
 
-    def sources(self):
-        tp, zhi = lax.div(self.tok, 2), lax.rem(self.tok, 2)
-        return [(self.tok_of(y, zhi, (1 - self.core) * 2 + self.par), tp) for y in range(SIDE)]
-
 
 XY = [(dy, dx) for dy in range(SIDE) for dx in range(SIDE) if (dy, dx) != (0, 0)]
 
@@ -276,7 +272,6 @@
         copy.start()
     targets = [grid.at_xy(*d) for d in XY] + [grid.sibling(), grid.pair()]
     targets += [grid.on_line(d) for d in range(1, DEPTH // 2)] + [grid.on_ring(d) for d in (4, 8, 12, 1, -1, -2)]
-    targets += grid.sources()
     barrier = pltpu.get_barrier_semaphore()
     for device in targets:
         pl.semaphore_signal(barrier, inc=1, device_id=device, device_id_type=pl.DeviceIdType.MESH)

time: 141 us -> 140 us (level)
  no operation moved by 1% of the time
where the time goes in v5:
time: 140 us
  Pallas kernels  136 us (97%)
  local copies, waits for them, and re-layouts  3.01 us (2%)
    pallas_call x1, Pallas kernels, per_device(): pl.pallas_call(functools.partial(kernel, scale, cols), name='step', out_s...  136 us
    unnamed x2, local copies, waits for them, and re-layouts  3.01 us

profile of v5, /device:TPU:1, one launch (start us, length us, event | category | flops | bytes accessed | tf_op | source)
XLA Modules:
  0.0 139.6 jit_solution(15101738359658386790)
XLA Ops:
  0.6 136.0 %step.1 = (bf16[4,32,192]{2,1,0:T(8,128)(2,1)}, bf16[96,512]{1,0:T(8,128)(2,1)}) custom-call(bf16[4,32,512]{2,1,0:T(8,128)(2,1)} %refs_0_.1, bf16[4,32,192]{2,1,0:T(8,128)(2,1)} %refs_1_.1, bf16[4,32,3072]{2,1,0:T(8,128)(2,1)} %refs_2_.1, bf16[512,3072]{1,0:T(8,128)(2,1)} %refs_3_.1), custom_call_target="tpu_custom_call" | custom-call | tf_op jit(solution)/shard_map/step/pallas_call | solution.py:636
  136.6 1.5 %copy.8 = bf16[4,32,192]{2,1,0:T(8,128)(2,1)} copy(bf16[4,32,192]{2,1,0:T(8,128)(2,1)} %get-tuple-element.8) | data formatting | bytes 98304
  138.1 1.5 %copy.9 = bf16[512,96]{0,1:T(8,128)(2,1)} copy(bf16[512,96]{0,1:T(8,128)(2,1)} %bitcast.1) | data formatting | bytes 196608
